TPU v7x, 32 devices: a whole 2x2x4 slice. The times are simulated.
32 devices in a mesh: ctx: 16 (over z, y, core), tp: 2 (over x).
Axes of the slice: x: 2, y: 2, z: 4, core: 2. Of those that a mesh axis runs over, the one named last changes fastest.
Arguments:
- queries: bfloat16 [4096, 4096], P('ctx', 'tp'), may hold values from -5 to 5
- key_head_array: bfloat16 [4096, 1024], P('ctx', 'tp'), may hold values from -8 to 8
- value_head_array: bfloat16 [4096, 1024], P('ctx', 'tp'), may hold values from -6 to 6
- ssm_input: bfloat16 [4096, 4096], P('ctx', 'tp'), may hold values from -6 to 6
- ssm_gate: bfloat16 [4096, 4096], P('ctx', 'tp'), may hold values from -30 to 30
- ssm_write: bfloat16 [4096, 1024], P('ctx', 'tp'), may hold values from -2.5 to 2.5
- ssm_read: bfloat16 [4096, 1024], P('ctx', 'tp'), may hold values from -2.5 to 2.5
- step_size: float32 [64, 4096], P('tp', 'ctx'), may hold values from 0.005 to 0.1
- log_decay: float32 [64, 4096], P('tp', 'ctx'), may hold values from -1 to 0
- skip_gain: float32 [64], P('tp'), may hold values from 0.5 to 2
- norm_gain: float32 [4096], P('tp'), may hold values from 0.1 to 1.9
- out_weight: bfloat16 [4096, 2048], P('tp'), may hold values from -2 to 2
Outputs:
- attn_mixed: float32 [4096, 2048], P('ctx', 'tp')
- ssm_output: float32 [4096, 4096], P('ctx', 'tp')
All inputs are finite; a program needn't handle non-finite values.
Results may differ from a plain program's by a relative error of at most 0.0053.
Values may be sent and summed in bfloat16 or wider, within the bound.
No kernel may reach another device: no remote copies, remote signals or barrier semaphores. Data moves between devices by JAX's collectives and lax.ppermute only.
A program may use at most 128 MiB of HBM per device.

v0:
```python
import math

import jax
import jax.numpy as jnp
from jax import lax
from jax.sharding import PartitionSpec as P

HEAD_SIZE = 128
P_SIZE = 64
NS = 128


neg_big = -1e30


def prefix_2(x, axis, combine, identity, reverse):
    count, mine = (lax.axis_size(axis), lax.axis_index(axis))
    everything = jax.tree.map(lambda part: lax.all_gather(part, axis), x)
    start = jax.tree.map(
        lambda part, zero: jnp.broadcast_to(jnp.asarray(zero, part.dtype), part.shape), x, identity
    )

    def lap(k, before):
        at = count - 1 - k if reverse else k
        reached = at > mine if reverse else at < mine
        new = combine(before, jax.tree.map(lambda part: part[at], everything))
        return jax.tree.map(lambda a, b: jnp.where(reached, a, b), new, before)

    return lax.fori_loop(0, count, lap, start)


def broadcast(x, axis, root):
    mine = lax.axis_index(axis) == root
    return lax.psum(jnp.where(mine, x, jnp.zeros_like(x)), axis)


def online_update(running, query_blk, key_blk, value_blk, query_pos, key_pos, score_scale):
    top_old, total_old, acc_old = running
    scores = (
        jnp.einsum("qgrd,kgd->grqk", query_blk, key_blk, preferred_element_type=jnp.float32)
        * score_scale
    )
    allowed = key_pos[None, None, None, :] <= query_pos[None, None, :, None]
    top_block = jnp.max(jnp.where(allowed, scores, neg_big), axis=-1)
    top_new = jnp.maximum(top_old, top_block)
    weights = jnp.where(allowed, jnp.exp(scores - top_new[..., None]), 0.0)
    factor = jnp.exp(top_old - top_new)
    total_new = total_old * factor + jnp.sum(weights, axis=-1)
    acc_new = acc_old * factor[..., None] + jnp.einsum(
        "grqk,kgd->grqd",
        weights.astype(jnp.bfloat16),
        value_blk,
        preferred_element_type=jnp.float32,
    )
    return (top_new, total_new, acc_new)


def compose(earlier, later):
    return (earlier[0] * later[0], later[0][..., None, None] * earlier[1] + later[1])


def steps_for():
    return 4


def body(
    queries,
    key_head_array,
    value_head_array,
    ssm_input,
    ssm_gate,
    ssm_write,
    ssm_read,
    step_size,
    log_decay,
    skip_gain,
    norm_gain,
    out_weight,
):
    ctx_count = lax.axis_size("ctx")
    ctx_index = lax.axis_index("ctx")
    tok_dev = queries.shape[0]
    half = tok_dev // 2
    kv_dev = key_head_array.shape[1] // HEAD_SIZE
    heads_dev = queries.shape[1] // HEAD_SIZE
    group_repeat = heads_dev // kv_dev
    score_scale = 1.0 / math.sqrt(HEAD_SIZE)
    last_block = 2 * ctx_count - 1
    row_ids = jnp.arange(half, dtype=jnp.int32)
    early_qpos = ctx_index * half + row_ids
    late_qpos = (last_block - ctx_index) * half + row_ids
    query_early = queries[:half].reshape(half, kv_dev, group_repeat, HEAD_SIZE)
    query_late = queries[half:].reshape(half, kv_dev, group_repeat, HEAD_SIZE)

    def fresh_state():
        return (
            jnp.full((kv_dev, group_repeat, half), neg_big, jnp.float32),
            jnp.zeros((kv_dev, group_repeat, half), jnp.float32),
            jnp.zeros((kv_dev, group_repeat, half, HEAD_SIZE), jnp.float32),
        )

    key_piece = lax.all_gather(key_head_array, "ctx", axis=0, tiled=True)
    value_piece = lax.all_gather(value_head_array, "ctx", axis=0, tiled=True)
    shard_count = key_piece.shape[0] // tok_dev
    per_step = steps_for()
    turns = shard_count // per_step
    key_groups = key_piece.reshape(turns, per_step, 2, half, kv_dev, HEAD_SIZE)
    value_groups = value_piece.reshape(turns, per_step, 2, half, kv_dev, HEAD_SIZE)

    def one_turn(running_pair, inputs):
        key_grp, value_grp, turn_index = inputs
        base_shard = turn_index * per_step
        shard_ids = base_shard + jnp.arange(per_step, dtype=jnp.int32)
        early_kpos = (shard_ids[:, None] * half + row_ids[None, :]).reshape(-1)
        late_kpos = ((last_block - shard_ids)[:, None] * half + row_ids[None, :]).reshape(-1)
        early_keys = key_grp[:, 0].reshape(per_step * half, kv_dev, HEAD_SIZE)
        late_keys = key_grp[:, 1].reshape(per_step * half, kv_dev, HEAD_SIZE)
        early_vals = value_grp[:, 0].reshape(per_step * half, kv_dev, HEAD_SIZE)
        late_vals = value_grp[:, 1].reshape(per_step * half, kv_dev, HEAD_SIZE)
        run_early, run_late = running_pair
        run_early = lax.cond(
            base_shard <= ctx_index,
            lambda running_now: online_update(
                running_now,
                query_early,
                early_keys,
                early_vals,
                early_qpos,
                early_kpos,
                score_scale,
            ),
            lambda running_now: running_now,
            run_early,
        )
        run_late = online_update(
            run_late, query_late, early_keys, early_vals, late_qpos, early_kpos, score_scale
        )
        run_late = lax.cond(
            base_shard + per_step - 1 >= ctx_index,
            lambda running_now: online_update(
                running_now, query_late, late_keys, late_vals, late_qpos, late_kpos, score_scale
            ),
            lambda running_now: running_now,
            run_late,
        )
        return ((run_early, run_late), None)

    result_pair, unused_out = lax.scan(
        one_turn,
        (fresh_state(), fresh_state()),
        (key_groups, value_groups, jnp.arange(turns, dtype=jnp.int32)),
    )

    def finish(running):
        top_fin, total_fin, acc_fin = running
        heads_out = acc_fin / total_fin[..., None]
        return (
            jnp.transpose(heads_out, (2, 0, 1, 3))
            .reshape(half, heads_dev * HEAD_SIZE)
            .astype(jnp.bfloat16)
        )

    attn_heads = jnp.concatenate([finish(result_pair[0]), finish(result_pair[1])], axis=0)
    head_terms = jnp.dot(attn_heads, out_weight, preferred_element_type=jnp.float32)
    attn_mixed = lax.psum_scatter(head_terms, "tp", scatter_dimension=1, tiled=True)
    heads_ssm = step_size.shape[0]
    groups_dev = ssm_write.shape[1] // NS
    per_group = heads_ssm // groups_dev
    causal = row_ids[:, None] >= row_ids[None, :]
    skip_cols = skip_gain.reshape(groups_dev, per_group)
    gain_cols = norm_gain.reshape(groups_dev, per_group * P_SIZE)

    def block_parts(row_from):
        cum_decay = jnp.cumsum(log_decay[:, row_from : row_from + half], axis=1).reshape(
            groups_dev, per_group, half
        )
        step_blk = step_size[:, row_from : row_from + half].reshape(groups_dev, per_group, half)
        input_blk = ssm_input[row_from : row_from + half].reshape(
            half, groups_dev, per_group, P_SIZE
        )
        write_blk = ssm_write[row_from : row_from + half].reshape(half, groups_dev, NS)
        read_blk = ssm_read[row_from : row_from + half].reshape(half, groups_dev, NS)
        scaled = (
            input_blk.astype(jnp.float32) * jnp.transpose(step_blk, (2, 0, 1))[..., None]
        ).astype(jnp.bfloat16)
        inner_prod = jnp.einsum(
            "tgn,sgn->gts", read_blk, write_blk, preferred_element_type=jnp.float32
        )
        decay_gap = cum_decay[..., :, None] - cum_decay[..., None, :]
        mixing = jnp.where(
            causal, inner_prod[:, None] * jnp.exp(jnp.where(causal, decay_gap, 0.0)), 0.0
        ).astype(jnp.bfloat16)
        local_out = jnp.einsum(
            "gjts,sgjp->tgjp", mixing, scaled, preferred_element_type=jnp.float32
        )
        tail_decay = jnp.exp(cum_decay[..., -1:] - cum_decay)
        written = (
            jnp.transpose(write_blk, (1, 0, 2)).astype(jnp.float32)[:, None] * tail_decay[..., None]
        ).astype(jnp.bfloat16)
        block_state = jnp.einsum(
            "sgjp,gjsn->gjpn", scaled, written, preferred_element_type=jnp.float32
        )
        block_decay = jnp.exp(cum_decay[..., -1])
        return ((block_decay, block_state), (local_out, cum_decay, read_blk, input_blk, row_from))

    def block_output(entering, pieces):
        local_out, cum_decay, read_blk, input_blk, row_from = pieces
        carried = jnp.einsum(
            "tgn,gjpn->tgjp",
            read_blk.astype(jnp.float32),
            entering,
            precision=lax.Precision.HIGHEST,
        )
        mixed_out = (
            local_out
            + carried * jnp.transpose(jnp.exp(cum_decay), (2, 0, 1))[..., None]
            + skip_cols[None, :, :, None] * input_blk.astype(jnp.float32)
        )
        gate_blk = ssm_gate[row_from : row_from + half].reshape(
            half, groups_dev, per_group * P_SIZE
        )
        gated = mixed_out.reshape(half, groups_dev, per_group * P_SIZE) * jax.nn.silu(
            gate_blk.astype(jnp.float32)
        )
        mean_square = jnp.mean(gated * gated, axis=-1, keepdims=True)
        normed = gated * lax.rsqrt(mean_square + 1e-05) * gain_cols[None]
        return normed.reshape(half, heads_ssm * P_SIZE)

    early_elem, early_rest = block_parts(0)
    late_elem, late_rest = block_parts(half)
    unit_decay = jnp.ones((groups_dev, per_group), jnp.float32)
    zero_state = jnp.zeros((groups_dev, per_group, P_SIZE, NS), jnp.float32)
    prefix = prefix_2(
        (early_elem[0], early_elem[1]), "ctx", compose, (unit_decay, zero_state), False
    )
    inclusive = compose(prefix, early_elem)
    total_state = broadcast(inclusive[1], "ctx", ctx_count - 1)
    suffix = prefix_2((late_elem[0], late_elem[1]), "ctx", compose, (unit_decay, zero_state), True)
    late_entering = suffix[0][..., None, None] * total_state + suffix[1]
    ssm_output = jnp.concatenate(
        [block_output(prefix[1], early_rest), block_output(late_entering, late_rest)], axis=0
    )
    return (attn_mixed, ssm_output)


def solution(mesh):
    placed = (
        P("ctx", "tp"),
        P("ctx", "tp"),
        P("ctx", "tp"),
        P("ctx", "tp"),
        P("ctx", "tp"),
        P("ctx", "tp"),
        P("ctx", "tp"),
        P("tp", "ctx"),
        P("tp", "ctx"),
        P("tp"),
        P("tp"),
        P("tp", None),
    )
    return jax.shard_map(
        body,
        mesh=mesh,
        in_specs=placed,
        out_specs=(P("ctx", "tp"), P("ctx", "tp")),
        check_vma=False,
    )
```

profile of v0, /device:TPU:0, one launch (start us, length us, event | category | flops | bytes accessed | tf_op | source)
XLA Modules:
  0.0 505.0 jit_solution(12839579409607009505)
XLA Ops:
  17.8 1.8 fusion.66
  19.7 2.2 reduce_window_sum.24
  24.7 2.5 fusion.67
  33.9 1.7 copy.166
  36.9 2.2 fusion.92
  42.0 24.4 %all-gather = f32[64,8,1]{1,2,0:T(1,128)} all-gather(f32[4,8,1]{1,2,0:T(1,128)} %bitcast.327), channel_id=2, replica_groups=mesh['ctx'=16,'tp'=2] {'ctx'}, dimensions={0}, use_global_device_ids=true | all-gather | bytes 2176 | tf_op jit(solution)/shard_map/all_gather | solution.py:18
  66.4 19.0 %all-gather.2 = f32[64,8,1]{1,2,0:T(1,128)} all-gather(f32[4,8,1]{1,2,0:T(1,128)} %bitcast.328), channel_id=4, replica_groups=mesh['ctx'=16,'tp'=2] {'ctx'}, dimensions={0}, use_global_device_ids=true | all-gather | bytes 2176 | tf_op jit(solution)/shard_map/all_gather | solution.py:18
  87.9 2.7 convolution_bitcast_fusion.2
  90.7 1.9 convolution_bitcast_fusion.3
  92.6 7.0 %reshape.295 = bf16[4,4,2,128,4,128]{5,4,3,2,1,0:T(4,128)(2,1)} reshape(bf16[4096,512]{1,0:T(8,128)(2,1)} %all-gather.9.cloned.1.call-done) | data formatting | bytes 8388608 | tf_op jit(solution)/shard_map/reshape | solution.py:107
  99.5 15.5 %all-gather.11.cloned.1.call-done = bf16[4096,512]{1,0:T(8,128)(2,1)} async-done(((bf16[256,512]{1,0:T(8,128)(2,1)}), bf16[4096,512]{1,0:T(8,128)(2,1)}) %all-gather.11.cloned.1.call-update) | async-done | bytes 4194320 | tf_op jit(solution)/shard_map/all_gather | solution.py:103
  115.0 6.9 %reshape.296 = bf16[4,4,2,128,4,128]{5,4,3,2,1,0:T(4,128)(2,1)} reshape(bf16[4096,512]{1,0:T(8,128)(2,1)} %all-gather.11.cloned.1.call-done) | data formatting | bytes 8388608 | tf_op jit(solution)/shard_map/reshape | solution.py:108
  124.1 57.9 %while.58 = (s32[]{:T(128)}, f32[4,4,128]{2,1,0:T(4,128)S(1)}, f32[4,4,128]{2,1,0:T(4,128)S(1)}, f32[4,4,128,128]{3,2,1,0:T(8,128)}, f32[4,4,128]{2,1,0:T(4,128)...) while((s32[]{:T(128)}, f32[4,4,128]{2,1,0:T(4,128)S(1)}, ...), condition=%wide.region_11.12_spmd.clone.clone, body=%wide.region_0.11_spmd.clone.clone.sunk | while | flops 1646999296 | bytes 91899224 | solution.py:148
  125.7 2.3 constant_dynamic-slice_fusion.3
  130.3 1.5 fusion.129
  132.8 4.5 conditional.9
  134.8 1.5 fusion.36
  137.3 5.6 %conditional.8 = ((f32[4,4,128]{2,1,0:T(4,128)S(1)}, f32[4,4,128]{2,1,0:T(4,128)S(1)}, f32[4,4,128,128]{3,2,1,0:T(8,128)})) conditional(s32[]{:T(128)} %convert_element_type.198, (f32[4,4,128]{2,1,0:T(4,128)S(1)}, f32[4,4,128]{2,1,0:T(4,128)S(1)}, f32[4,4,128,128]{3,2,1,0:T(8,128)}) %tuple.174, (s32[4]{0:T(128)S(1)}, s32[128]{0:T(128)S(1)}, ...), branch_computations={%region_1.1_spmd, %region_2.4_spmd} | conditional | flops 548999808 | bytes 27138184 | solution.py:121
  137.5 1.9 fusion.6
  140.3 1.5 fusion.17
  144.3 2.3 constant_dynamic-slice_fusion.3
  151.4 4.5 conditional.9
  153.4 1.5 fusion.36
  157.3 2.3 constant_dynamic-slice_fusion.3
  161.9 1.5 fusion.129
  164.4 4.5 conditional.9
  166.4 1.5 fusion.36
  170.4 2.3 constant_dynamic-slice_fusion.3
  174.9 1.5 fusion.129
  177.4 4.5 conditional.9
  179.4 1.5 fusion.36
  181.9 1.7 copy.117
  183.6 1.6 copy.118
  186.4 56.2 %all-gather.13.cloned.1.call-done = f32[64,8,64,128]{3,2,1,0:T(8,128)} async-done(((f32[4,8,64,128]{3,2,1,0:T(8,128)}), f32[64,8,64,128]{3,2,1,0:T(8,128)}) %all-gather.13.cloned.1.call-update) | async-done | bytes 16777232 | tf_op jit(solution)/shard_map/all_gather | solution.py:18
  242.6 34.7 %while.59 = (s32[]{:T(128)}, f32[4,8,64,128]{3,2,1,0:T(8,128)S(1)}, s32[]{:T(128)}, f32[16,4,8]{2,1,0:T(4,128)}, f32[16,4,8,64,128]{4,3,2,1,0:T(8,128)}, /*index=5*/s32[]{:T(128)}, s32[]{:T(128)}) while((s32[]{:T(128)}, f32[4,8,64,128]{3,2,1,0:T(8,128)S(1)}, s32[]{:T(128)}, f32[16,4,8]{2,1,0:T(4,128)}, ...), condition=%wide.region_15.16_spmd.clone, body=%wide.region_14.15_spmd.clone.sunk | while | flops 1048580 | bytes 3146217 | solution.py:29
  249.7 1.6 fusion.130
  252.0 1.7 fusion.130
  278.7 7.2 %fusion.68 = f32[256,2048]{1,0:T(8,128)} fusion(bf16[2048,2048]{1,0:T(8,128)(2,1)} %param.33, bf16[128,2048]{0,1:T(8,128)(2,1)S(1)} %bitcast.292, bf16[128,2048]{0,1:T(8,128)(2,1)S(1)} %bitcast.293), kind=kOutput, calls=%fused_computation.96 | convolution fusion | flops 2149580800 | bytes 11534336 | tf_op jit(solution)/shard_map/dot_general | solution.py:164
  285.9 83.8 %all-gather.15.cloned.1.call-done = f32[64,8,64,128]{3,2,1,0:T(8,128)} async-done(((f32[4,8,64,128]{3,2,1,0:T(8,128)}), f32[64,8,64,128]{3,2,1,0:T(8,128)}) %all-gather.15.cloned.1.call-update) | async-done | bytes 16777232 | tf_op jit(solution)/shard_map/all_gather | solution.py:18
  369.7 34.7 %while.60 = (s32[]{:T(128)}, f32[4,8]{1,0:T(4,128)S(1)}, f32[4,8,64,128]{3,2,1,0:T(8,128)S(1)}, s32[]{:T(128)}, f32[16,4,8]{2,1,0:T(4,128)}, /*index=5*/f32[16,4...) while((s32[]{:T(128)}, f32[4,8]{1,0:T(4,128)S(1)}, ...), condition=%wide.region_19.20_spmd.clone, body=%wide.region_18.19_spmd.clone.sunk | while | flops 1048680 | bytes 3146545 | solution.py:29
  404.5 3.5 multiply_reduce_fusion.1
  408.7 2.5 copy.128
  411.2 53.2 %all-reduce.2.cloned.1.call-done = f32[4,8,64,128]{3,2,1,0:T(8,128)} async-done(((f32[4,8,64,128]{3,2,1,0:T(8,128)}), f32[4,8,64,128]{3,2,1,0:T(8,128)}) %all-reduce.2.cloned.1.call-update) | async-done | bytes 1048592 | tf_op jit(solution)/shard_map/psum | solution.py:34
  464.4 3.9 multiply_reduce_fusion
  470.0 2.5 copy.140
  472.6 2.4 multiply_multiply_fusion.1
  474.9 1.5 pad_maximum_fusion
  476.5 21.7 %reduce-scatter.2.cloned.1.call-done = f32[256,1024]{1,0:T(8,128)} async-done(((f32[256,2048]{1,0:T(8,128)}), f32[256,1024]{1,0:T(8,128)}) %reduce-scatter.2.cloned.1.call-update) | async-done | bytes 1048592 | tf_op jit(solution)/shard_map/reduce_scatter | solution.py:165
  (339 shorter events, 130.4 us)
Async XLA Ops:
  7.2 85.4 %all-gather.9.cloned.1.call-start = ((), (), s32[]{:S(2)}) async-start(), calls=%async_computation.1 | async-start | bytes 4456448 | tf_op jit(solution)/shard_map/all_gather | solution.py:102
  7.9 107.1 %all-gather.11.cloned.1.call-start = ((), (), s32[]{:S(2)}) async-start(), calls=%async_computation.2 | async-start | bytes 4456448 | tf_op jit(solution)/shard_map/all_gather | solution.py:103
  8.6 233.9 %all-gather.13.cloned.1.call-start = ((), (), s32[]{:S(2)}) async-start(), calls=%async_computation.5 | async-start | bytes 17825792 | tf_op jit(solution)/shard_map/all_gather | solution.py:18
  13.6 77.0 %copy-start.5 = (f32[128,2048]{0,1:T(8,128)}, f32[128,2048]{0,1:T(8,128)S(1)}, u32[]{:S(2)}) copy-start(f32[128,2048]{0,1:T(8,128)S(1)} %copy.119) | copy-start | bytes 3145732
  16.6 6.4 %copy-start.23 = (f32[128,4,8]{0,2,1:T(8,128)}, f32[128,4,8]{0,2,1:T(8,128)S(1)}, u32[]{:S(2)}) copy-start(f32[128,4,8]{0,2,1:T(8,128)S(1)} %get-tuple-element.990) | copy-start | bytes 49156
  19.6 350.1 %all-gather.15.cloned.1.call-start = ((), (), s32[]{:S(2)}) async-start(), calls=%async_computation.6 | async-start | bytes 17825792 | tf_op jit(solution)/shard_map/all_gather | solution.py:18
  21.9 1.1 copy-start.22
  23.0 6.7 %copy-start.7 = (f32[128,2048]{0,1:T(8,128)}, f32[128,2048]{0,1:T(8,128)S(1)}, u32[]{:S(2)}) copy-start(f32[128,2048]{0,1:T(8,128)S(1)} %copy.131) | copy-start | bytes 3145732
  23.0 5.5 %copy-start.26 = (f32[4,8,1]{1,0,2:T(4,128)S(1)}, f32[4,8,1]{1,0,2:T(4,128)}, u32[]{:S(2)}) copy-start(f32[4,8,1]{1,0,2:T(4,128)} %copy.171) | copy-start | bytes 388
  23.0 6.0 %copy-start.21 = (bf16[256,512]{1,0:T(8,128)(2,1)S(1)}, bf16[256,512]{1,0:T(8,128)(2,1)}, u32[]{:S(2)}) copy-start(bf16[256,512]{1,0:T(8,128)(2,1)} %param.28) | copy-start | bytes 786436
  27.3 437.2 %all-reduce.2.cloned.1.call-start = ((), (), s32[]{:S(2)}) async-start(), calls=%async_computation.4 | async-start | bytes 2097152 | tf_op jit(solution)/shard_map/psum | solution.py:34
  36.9 51.0 %copy-start.8 = (f32[128,2048]{0,1:T(8,128)S(1)}, f32[128,2048]{0,1:T(8,128)}, u32[]{:S(2)}) copy-start(f32[128,2048]{0,1:T(8,128)} %copy-done.7) | copy-start | bytes 3145732
  42.0 48.7 %copy-start.24 = (f32[128,4,8]{0,2,1:T(8,128)S(1)}, f32[128,4,8]{0,2,1:T(8,128)}, u32[]{:S(2)}) copy-start(f32[128,4,8]{0,2,1:T(8,128)} %copy-done.23) | copy-start | bytes 49156
  129.1 1.2 copy-start.13
  130.3 1.5 copy-start.2
  131.8 1.0 copy-start.14
  133.1 1.7 copy-start.15
  137.5 2.8 copy-start.3
  137.5 2.8 copy-start.11
  147.6 1.2 copy-start.13
  148.8 1.5 copy-start.2
  151.7 1.7 copy-start.15
  160.7 1.2 copy-start.13
  161.9 1.5 copy-start.2
  163.4 1.0 copy-start.14
  164.7 1.7 copy-start.15
  167.9 1.0 copy-start.16
  173.7 1.2 copy-start.13
  174.9 1.6 copy-start.2
  177.7 1.7 copy-start.15
  180.9 1.0 copy-start.16
  181.9 60.7 %copy-start = (f32[4,8,64,128]{3,2,1,0:T(8,128)S(1)}, f32[4,8,64,128]{3,2,1,0:T(8,128)}, u32[]{:S(2)}) copy-start(f32[4,8,64,128]{3,2,1,0:T(8,128)} %custom-call) | copy-start | bytes 3145732
  242.6 34.7 %copy-start.4 = (f32[4,8,64,128]{3,2,1,0:T(8,128)S(1)}, f32[4,8,64,128]{3,2,1,0:T(8,128)}, u32[]{:S(2)}) copy-start(f32[4,8,64,128]{3,2,1,0:T(8,128)} %fusion.66) | copy-start | bytes 3145732
  242.6 34.7 %copy-start.29 = (f32[4,8]{1,0:T(4,128)S(1)}, f32[4,8]{1,0:T(4,128)}, u32[]{:S(2)}) copy-start(f32[4,8]{1,0:T(4,128)} %bitcast_exponential_fusion) | copy-start | bytes 388
  277.3 1.3 copy-start.18
  277.3 1.4 copy-start.19
  278.5 219.7 %reduce-scatter.2.cloned.1.call-start = ((), (), s32[]{:S(2)}) async-start(), calls=%async_computation.3 | async-start | bytes 3145728 | tf_op jit(solution)/shard_map/reduce_scatter | solution.py:165
  278.7 91.0 %copy-start.1 = (f32[4,8,64,128]{3,2,1,0:T(8,128)S(1)}, f32[4,8,64,128]{3,2,1,0:T(8,128)}, u32[]{:S(2)}) copy-start(f32[4,8,64,128]{3,2,1,0:T(8,128)} %custom-call.2) | copy-start | bytes 3145732
  278.7 91.0 %copy-start.25 = (f32[4,8]{1,0:T(4,128)S(1)}, f32[4,8]{1,0:T(4,128)}, u32[]{:S(2)}) copy-start(f32[4,8]{1,0:T(4,128)} %custom-call.1) | copy-start | bytes 388
  369.7 34.8 %copy-start.6 = (f32[128,2048]{0,1:T(8,128)S(1)}, f32[128,2048]{0,1:T(8,128)}, u32[]{:S(2)}) copy-start(f32[128,2048]{0,1:T(8,128)} %copy-done.5) | copy-start | bytes 3145732
  369.7 34.8 %copy-start.20 = (bf16[128,512]{0,1:T(8,128)(2,1)S(1)}, bf16[128,512]{0,1:T(8,128)(2,1)}, u32[]{:S(2)}) copy-start(bf16[128,512]{0,1:T(8,128)(2,1)} %copy.166) | copy-start | bytes 393220
  369.7 34.8 %copy-start.27 = (f32[128,4,8]{0,2,1:T(8,128)S(1)}, f32[128,4,8]{0,2,1:T(8,128)}, u32[]{:S(2)}) copy-start(f32[128,4,8]{0,2,1:T(8,128)} %get-tuple-element.994) | copy-start | bytes 49156
  369.7 34.8 %copy-start.31 = (f32[4,8]{1,0:T(4,128)S(1)}, f32[4,8]{1,0:T(4,128)}, u32[]{:S(2)}) copy-start(f32[4,8]{1,0:T(4,128)} %mul.374) | copy-start | bytes 388
  408.0 56.5 %copy-start.9 = (f32[128,2048]{0,1:T(8,128)S(1)}, f32[128,2048]{0,1:T(8,128)}, u32[]{:S(2)}) copy-start(f32[128,2048]{0,1:T(8,128)} %copy-done.7) | copy-start | bytes 3145732
  408.0 56.5 %copy-start.28 = (f32[128,4,8]{0,2,1:T(8,128)S(1)}, f32[128,4,8]{0,2,1:T(8,128)}, u32[]{:S(2)}) copy-start(f32[128,4,8]{0,2,1:T(8,128)} %get-tuple-element.996) | copy-start | bytes 49156
  468.3 4.2 copy-start.10
  468.3 4.2 copy-start.17
  468.3 4.2 copy-start.30
  (5 other events, 4.9 us)
Sparse Core Ops, SparseCore 0:
  10.2 53.4 all-gather.8
  65.8 49.1 all-gather.10
  117.2 125.3 all-gather.12
  244.6 125.0 all-gather.14
  373.0 91.3 all-reduce.1
  467.1 31.0 reduce-scatter.1
where the time goes:
time: 509 us; the launch traced here: 505 us
  waiting for transfers between devices  232 us (46%)
  other arithmetic  82.9 us (16%)
  local copies, waits for them, and re-layouts  81.4 us (16%)
  matrix products  46.4 us (9%)
  blocking collectives  43.4 us (9%)
  between operations  14.5 us (3%)
    all_gather x2, waiting for transfers between devices, prefix_2(): everything = jax.tree.map(lambda part: lax.all_gather(part, axis), x)  140 us
    select_n x48, other arithmetic, lap(): return jax.tree.map(lambda a, b: jnp.where(reached, a, b), new, before)  57.9 us
    psum x1, waiting for transfers between devices, broadcast(): return lax.psum(jnp.where(mine, x, jnp.zeros_like(x)), axis)  53.2 us
    all_gather x2, blocking collectives, prefix_2(): everything = jax.tree.map(lambda part: lax.all_gather(part, axis), x)  43.4 us
    reduce_scatter x1, waiting for transfers between devices, body(): lax.psum_scatter(head_terms, 'tp', scatter_dimension=1, tiled=True)  21.7 us
    all_gather x1, waiting for transfers between devices, body(): value_piece = lax.all_gather(value_head_array, 'ctx', axis=0, tiled=True)  15.5 us
    dot_general x9, matrix products, online_update(): jnp.einsum('grqk,kgd->grqd', weights.astype(jnp.bfloat16), value_blk, pre...  13.6 us
    dynamic_slice x16, local copies, waits for them, and re-layouts, body(): lax.scan(one_turn, (fresh_state(), fresh_state()), (key_groups, value_gro...  13.4 us
  transfers between devices with their start and end apart: 6, of which 5 were waited for; matrix products, arithmetic and copies ran while one was open for 40% of the time, Pallas kernels for 0%

commit v1 on v0

--- a/solution.py
+++ b/solution.py
@@ -1,8 +1,11 @@
+import functools
 import math
 
 import jax
 import jax.numpy as jnp
 from jax import lax
+from jax.experimental import pallas as pl
+from jax.experimental.pallas import tpu as pltpu
 from jax.sharding import PartitionSpec as P
 
 HEAD_SIZE = 128
@@ -171,9 +174,11 @@
     gain_cols = norm_gain.reshape(groups_dev, per_group * P_SIZE)
 
     def block_parts(row_from):
-        cum_decay = jnp.cumsum(log_decay[:, row_from : row_from + half], axis=1).reshape(
-            groups_dev, per_group, half
-        )
+        cum_decay = jnp.dot(
+            log_decay[:, row_from : row_from + half],
+            (row_ids[:, None] <= row_ids[None, :]).astype(jnp.float32),
+            precision=lax.Precision.HIGHEST,
+        ).reshape(groups_dev, per_group, half)
         step_blk = step_size[:, row_from : row_from + half].reshape(groups_dev, per_group, half)
         input_blk = ssm_input[row_from : row_from + half].reshape(
             half, groups_dev, per_group, P_SIZE
@@ -241,6 +246,409 @@
         [block_output(prefix[1], early_rest), block_output(late_entering, late_rest)], axis=0
     )
     return (attn_mixed, ssm_output)
+
+
+LOG2E = 1.4426950408889634
+F32 = jnp.float32
+BF16 = jnp.bfloat16
+HIGH = lax.Precision.HIGHEST
+NT = (((1,), (1,)), ((), ()))
+TN = (((0,), (0,)), ((), ()))
+VMEM_SPEC = pl.BlockSpec(memory_space=pltpu.VMEM)
+
+
+def expand_pairs(cols, pair):
+    rows = cols.shape[0]
+    lane = lax.broadcasted_iota(jnp.int32, (rows, 2 * P_SIZE), 1)
+    first, second = cols[:, 2 * pair : 2 * pair + 1], cols[:, 2 * pair + 1 : 2 * pair + 2]
+    return jnp.where(lane < P_SIZE, first, second)
+
+
+def ssm_local_kernel(x_ref, write_ref, read_ref, step_ref, ldc_ref, ldr_ref, skip_ref, mixed_ref, state_ref):
+    span = x_ref.shape[0]
+    per_group = step_ref.shape[2]
+    row = lax.broadcasted_iota(jnp.int32, (span, span), 0)
+    col = lax.broadcasted_iota(jnp.int32, (span, span), 1)
+    causal = col <= row
+    tri = causal.astype(F32)
+    ldc, ldr, step = ldc_ref[0], ldr_ref[0], step_ref[0]
+    cum_c = jnp.dot(tri, ldc, precision=HIGH, preferred_element_type=F32)
+    cum_r = lax.dot_general(ldr, tri, NT, precision=HIGH, preferred_element_type=F32)
+    write, read = write_ref[...], read_ref[...]
+    inner = lax.dot_general(read, write, NT, preferred_element_type=F32)
+    last = cum_c[span - 1 : span, :]
+    tail = jnp.exp(last - cum_c)
+    lane = lax.broadcasted_iota(jnp.int32, (span, 2 * P_SIZE), 1)
+    weighted = []
+    for pair in range(per_group // 2):
+        cols = pl.ds(pair * 2 * P_SIZE, 2 * P_SIZE)
+        x = x_ref[:, cols].astype(F32)
+        scaled = (x * expand_pairs(step, pair)).astype(BF16)
+        mixes = []
+        for head in (2 * pair, 2 * pair + 1):
+            gap = cum_c[:, head : head + 1] - cum_r[head : head + 1, :]
+            decay = jnp.exp(jnp.where(causal, gap, 0.0))
+            mixes.append(jnp.where(causal, inner * decay, 0.0).astype(BF16))
+        zero = jnp.zeros_like(scaled)
+        stacked = jnp.concatenate(
+            [jnp.where(lane < P_SIZE, scaled, zero), jnp.where(lane >= P_SIZE, scaled, zero)], axis=0
+        )
+        local = jnp.dot(jnp.concatenate(mixes, axis=1), stacked, preferred_element_type=F32)
+        mixed_ref[:, cols] = local + skip_ref[0, :, cols] * x
+        weighted.append((scaled.astype(F32) * expand_pairs(tail, pair)).astype(BF16))
+        state_ref[0, pl.ds(NS, 8), cols] = jnp.broadcast_to(expand_pairs(last, pair), (8, 2 * P_SIZE))
+    state_ref[0, pl.ds(0, NS), :] = lax.dot_general(
+        write, jnp.concatenate(weighted, axis=1), TN, preferred_element_type=F32
+    )
+
+
+def ssm_out_kernel(mixed_ref, read_ref, ldc_ref, enter_ref, gate_ref, gain_ref, out_ref):
+    span = mixed_ref.shape[0]
+    row = lax.broadcasted_iota(jnp.int32, (span, span), 0)
+    col = lax.broadcasted_iota(jnp.int32, (span, span), 1)
+    tri = (col <= row).astype(F32)
+    cum_c = jnp.dot(tri, ldc_ref[0], precision=HIGH, preferred_element_type=F32)
+    grow = jnp.exp(cum_c)
+    carried = jnp.dot(read_ref[...], enter_ref[0], preferred_element_type=F32)
+    grown = jnp.concatenate([expand_pairs(grow, pair) for pair in range(grow.shape[1] // 2)], axis=1)
+    gate = gate_ref[...].astype(F32)
+    gated = (mixed_ref[...] + carried * grown) * (gate / (1.0 + jnp.exp(-gate)))
+    mean_square = jnp.mean(gated * gated, axis=1, keepdims=True)
+    out_ref[...] = gated * lax.rsqrt(mean_square + 1e-05) * gain_ref[0]
+
+
+def attend_tile(q, keys, values_t, running, allowed):
+    m_old, l_old, acc_old = running
+    c = LOG2E / math.sqrt(HEAD_SIZE)
+    s = lax.dot_general(keys, q, NT, preferred_element_type=F32)
+    if allowed is not None:
+        s = jnp.where(allowed, s, neg_big)
+    m_new = jnp.max(s, axis=0, keepdims=True)
+    if m_old is not None:
+        m_new = jnp.maximum(m_old, m_new)
+    p = jnp.exp2((s - m_new) * c)
+    l_new = jnp.sum(p, axis=0, keepdims=True)
+    acc_new = jnp.dot(values_t, p.astype(BF16), preferred_element_type=F32)
+    if m_old is not None:
+        alpha = jnp.exp2((m_old - m_new) * c)
+        l_new = l_new + alpha * l_old
+        acc_new = acc_new + alpha * acc_old
+    return m_new, l_new, acc_new
+
+
+def plane_rows(ref, which, half, span):
+    return ref[:, which, :, pl.ds(half * span, span), :].reshape(4 * span, HEAD_SIZE)
+
+
+def query_tile(q_ref, turn, half, head, span):
+    return q_ref[turn, :, pl.ds(half * span, span), pl.ds(head * HEAD_SIZE, HEAD_SIZE)].reshape(2 * span, HEAD_SIZE)
+
+
+def attn_local_kernel(place_ref, q_ref, kv_ref, *rest):
+    stat_ref, acc_ref = rest[-2:]
+    y, core = place_ref[0], place_ref[1]
+    span = q_ref.shape[2] // 2
+    heads = q_ref.shape[3] // HEAD_SIZE
+    tile = 2 * span
+
+    def position(shape, dim, half):
+        at = lax.broadcasted_iota(jnp.int32, shape, dim)
+        block = jnp.where(at < span, core, 1 - core)
+        return (block if half == 0 else 1 - block) * span + at % span
+
+    def update(half, turn, head, keys, values_t, allowed, first):
+        where = pl.ds(pl.multiple_of(turn * tile, tile), tile)
+        running = (None, None, None)
+        if not first:
+            running = (
+                stat_ref[half, head, pl.ds(0, 1), where],
+                stat_ref[half, head, pl.ds(1, 1), where],
+                acc_ref[half, head, :, where],
+            )
+        running = attend_tile(query_tile(q_ref, turn, half, head, span), keys, values_t, running, allowed)
+        stat_ref[half, head, pl.ds(0, 1), where] = running[0]
+        stat_ref[half, head, pl.ds(1, 1), where] = running[1]
+        acc_ref[half, head, :, where] = running[2]
+
+    for half in range(2):
+        allowed = position((tile, 1), 0, half) <= position((1, tile), 1, half)
+        for turn in range(2):
+            keys = kv_ref[turn, 0, :, pl.ds(half * span, span), :].reshape(tile, HEAD_SIZE)
+            values_t = kv_ref[turn, 1, :, pl.ds(half * span, span), :].reshape(tile, HEAD_SIZE).T
+            for head in range(heads):
+                update(half, turn, head, keys, values_t, allowed, True)
+        after = 1 - y if half == 0 else y
+        keys = kv_ref[1 - after, 0, :, pl.ds(half * span, span), :].reshape(tile, HEAD_SIZE)
+        values_t = kv_ref[1 - after, 1, :, pl.ds(half * span, span), :].reshape(tile, HEAD_SIZE).T
+        for head in range(heads):
+            update(half, after, head, keys, values_t, None, False)
+    keys, values_t = plane_rows(kv_ref, 0, 0, span), plane_rows(kv_ref, 1, 0, span).T
+    for turn in range(2):
+        for head in range(heads):
+            update(1, turn, head, keys, values_t, None, False)
+
+
+def attn_remote_kernel(last, later_ref, q_ref, kv_ref, stat_in, acc_in, *rest):
+    if last:
+        out_ref, stat_ref, acc_ref = rest[-3:]
+    else:
+        stat_ref, acc_ref = rest[-2:]
+    later = later_ref[0]
+    span = q_ref.shape[2] // 2
+    heads = q_ref.shape[3] // HEAD_SIZE
+    tile = 2 * span
+    stat_ref[...] = stat_in[...]
+    acc_ref[...] = acc_in[...]
+
+    def unit(half, part):
+        keys, values_t = plane_rows(kv_ref, 0, part, span), plane_rows(kv_ref, 1, part, span).T
+        for turn in range(2):
+            where = pl.ds(turn * tile, tile)
+            for head in range(heads):
+                running = (
+                    stat_ref[half, head, pl.ds(0, 1), where],
+                    stat_ref[half, head, pl.ds(1, 1), where],
+                    acc_ref[half, head, :, where],
+                )
+                running = attend_tile(query_tile(q_ref, turn, half, head, span), keys, values_t, running, None)
+                stat_ref[half, head, pl.ds(0, 1), where] = running[0]
+                stat_ref[half, head, pl.ds(1, 1), where] = running[1]
+                acc_ref[half, head, :, where] = running[2]
+
+    unit(1, 0)
+    unit(later, later)
+    if last:
+        for half in range(2):
+            for head in range(heads):
+                scaled = acc_ref[half, head] / stat_ref[half, head, pl.ds(1, 1), :]
+                out_ref[:, :, pl.ds(half * span, span), pl.ds(head * HEAD_SIZE, HEAD_SIZE)] = scaled.T.reshape(
+                    2, 2, span, HEAD_SIZE
+                )
+
+
+def pack(state, log_row):
+    hi = lax.reduce_precision(log_row, 8, 7)
+    mid = lax.reduce_precision(log_row - hi, 8, 7)
+    row = lax.broadcasted_iota(jnp.int32, (16, state.shape[1]), 0)
+    rest = jnp.where(row == 0, hi, jnp.where(row == 1, mid, jnp.where(row == 2, log_row - hi - mid, 0.0)))
+    return jnp.concatenate([state.astype(BF16), rest.astype(BF16)], axis=0)
+
+
+def unpack(packed):
+    return packed[:NS].astype(F32), jnp.sum(packed[NS:].astype(F32), axis=0, keepdims=True)
+
+
+def chain(first, second):
+    return jnp.exp(second[1]) * first[0] + second[0], first[1] + second[1]
+
+
+def split_body(
+    queries,
+    key_head_array,
+    value_head_array,
+    ssm_input,
+    ssm_gate,
+    ssm_write,
+    ssm_read,
+    step_size,
+    log_decay,
+    skip_gain,
+    norm_gain,
+    out_weight,
+):
+    planes = lax.axis_size("ctx") // 4
+    ctx_index = lax.axis_index("ctx")
+    tp_index = lax.axis_index("tp")
+    z, y, core = ctx_index // 4, (ctx_index // 2) % 2, ctx_index % 2
+    tok_dev = queries.shape[0]
+    half = tok_dev // 2
+    group = queries.shape[1] // 4
+    everyone = range(4 * planes)
+    to_core = [(i, i ^ 1) for i in everyone]
+    to_y = [(i, i ^ 2) for i in everyone]
+
+    def send(x, pairs):
+        return lax.ppermute(x, "ctx", pairs)
+
+    def part(x, which, width, axis):
+        return lax.dynamic_slice_in_dim(x, which * width, width, axis)
+
+    def in_order(mine, other, at, axis=0):
+        return jnp.concatenate([jnp.where(at == 0, mine, other), jnp.where(at == 0, other, mine)], axis=axis)
+
+    def both(which):
+        return jnp.stack(
+            [part(key_head_array, which, 2 * HEAD_SIZE, 1), part(value_head_array, which, 2 * HEAD_SIZE, 1)]
+        )
+
+    kv_chip = jnp.stack([both(core), send(both(1 - core), to_core)], axis=1)
+    kv_own = jnp.stack(
+        [part(kv_chip, y, HEAD_SIZE, 3), send(part(kv_chip, 1 - y, HEAD_SIZE, 3), to_y)]
+    )
+    kv_from = [
+        send(kv_own, [(i, (i + 4 * turn) % (4 * planes)) for i in everyone]) for turn in range(1, planes)
+    ]
+
+    q_chip = jnp.stack([part(queries, core, 2 * group, 1), send(part(queries, 1 - core, 2 * group, 1), to_core)])
+    q_own = jnp.stack([part(q_chip, y, group, 2), send(part(q_chip, 1 - y, group, 2), to_y)])
+
+    groups = ssm_write.shape[1] // NS
+    per_group = step_size.shape[0] // groups
+    width = per_group * P_SIZE
+    by_group = (groups, per_group, tok_dev)
+    step_cols = jnp.transpose(step_size.reshape(by_group), (0, 2, 1))
+    ld_rows = log_decay.reshape(by_group)
+    ld_cols = jnp.transpose(ld_rows, (0, 2, 1))
+    skip_rows = jnp.repeat(skip_gain, P_SIZE).reshape(groups, 1, width)
+    gain_rows = norm_gain.reshape(groups, 1, width)
+    wide = pl.BlockSpec((half, width), lambda b, g: (b, g))
+    narrow = pl.BlockSpec((half, NS), lambda b, g: (b, g))
+    columns = pl.BlockSpec((1, half, per_group), lambda b, g: (g, b, 0))
+    per_row = pl.BlockSpec((1, 1, width), lambda b, g: (g, 0, 0))
+    mixed, states = pl.pallas_call(
+        ssm_local_kernel,
+        grid=(2, groups),
+        in_specs=[
+            wide,
+            narrow,
+            narrow,
+            columns,
+            columns,
+            pl.BlockSpec((1, per_group, half), lambda b, g: (g, 0, b)),
+            per_row,
+        ],
+        out_specs=[wide, pl.BlockSpec((1, NS + 8, width), lambda b, g: (b, 0, g))],
+        out_shape=[
+            jax.ShapeDtypeStruct((tok_dev, groups * width), F32),
+            jax.ShapeDtypeStruct((2, NS + 8, groups * width), F32),
+        ],
+        compiler_params=pltpu.CompilerParams(vmem_limit_bytes=32 * 2**20),
+        cost_estimate=pl.CostEstimate(flops=4 * 10**8, bytes_accessed=6 * 2**20, transcendentals=10**6),
+        name="ssm_local",
+    )(ssm_input, ssm_write, ssm_read, step_cols, ld_cols, ld_rows, skip_rows)
+
+    st_mine = part(states, core, 2 * width, 2)
+    st_other = send(part(states, 1 - core, 2 * width, 2), to_core)
+    st_zero, st_one = jnp.where(core == 0, st_mine, st_other), jnp.where(core == 0, st_other, st_mine)
+
+    def elem(packed):
+        return packed[:NS], packed[NS : NS + 1]
+
+    early_chip = chain(elem(st_zero[0]), elem(st_one[0]))
+    late_chip = chain(elem(st_one[1]), elem(st_zero[1]))
+    chip_pack = jnp.stack([pack(*early_chip), pack(*late_chip)])
+    cp_mine = part(chip_pack, y, width, 2)
+    cp_other = send(part(chip_pack, 1 - y, width, 2), to_y)
+    cp_zero, cp_one = jnp.where(y == 0, cp_mine, cp_other), jnp.where(y == 0, cp_other, cp_mine)
+    early_plane = chain(unpack(cp_zero[0]), unpack(cp_one[0]))
+    late_plane = chain(unpack(cp_one[1]), unpack(cp_zero[1]))
+    plane_pack = jnp.stack([pack(*early_plane), pack(*late_plane)])
+    plane_from = jnp.stack(
+        [plane_pack]
+        + [send(plane_pack, [(i, (i + 4 * turn) % (4 * planes)) for i in everyone]) for turn in range(1, planes)]
+    )
+
+    def of_plane(at):
+        return lax.dynamic_index_in_dim(plane_from, (z - at) % planes, 0, keepdims=False)
+
+    total = (jnp.zeros((NS, width), F32), jnp.zeros((1, width), F32))
+    enter_early = total[0]
+    for at in range(planes):
+        enter_early = jnp.where(z == at, total[0], enter_early)
+        total = chain(total, unpack(of_plane(at)[0]))
+    enter_late = total[0]
+    for at in range(planes - 1, -1, -1):
+        enter_late = jnp.where(z == at, total[0], enter_late)
+        total = chain(total, unpack(of_plane(at)[1]))
+
+    def step_on(state, packed):
+        block = unpack(packed)
+        return jnp.exp(block[1]) * state + block[0]
+
+    early_at = [enter_early, step_on(enter_early, cp_zero[0])]
+    late_at = [step_on(enter_late, cp_one[1]), enter_late]
+    chip_enter = [jnp.stack([early_at[k], late_at[k]]).astype(BF16) for k in range(2)]
+    ce_mine = jnp.where(y == 0, chip_enter[0], chip_enter[1])
+    ce_other = send(jnp.where(y == 0, chip_enter[1], chip_enter[0]), to_y)
+    ce = in_order(ce_mine, ce_other, y, axis=2).astype(F32)
+
+    def step_by(state, block):
+        return jnp.exp(block[1]) * state + block[0]
+
+    early_block = [ce[0], step_by(ce[0], elem(st_zero[0]))]
+    late_block = [step_by(ce[1], elem(st_one[1])), ce[1]]
+    block_enter = [jnp.stack([early_block[k], late_block[k]]).astype(BF16) for k in range(2)]
+    be_mine = jnp.where(core == 0, block_enter[0], block_enter[1])
+    be_other = send(jnp.where(core == 0, block_enter[1], block_enter[0]), to_core)
+    enter = in_order(be_mine, be_other, core, axis=2)
+
+    ssm_output = pl.pallas_call(
+        ssm_out_kernel,
+        grid=(2, groups),
+        in_specs=[
+            wide,
+            narrow,
+            columns,
+            pl.BlockSpec((1, NS, width), lambda b, g: (b, 0, g)),
+            wide,
+            per_row,
+        ],
+        out_specs=wide,
+        out_shape=jax.ShapeDtypeStruct((tok_dev, groups * width), F32),
+        compiler_params=pltpu.CompilerParams(vmem_limit_bytes=32 * 2**20),
+        cost_estimate=pl.CostEstimate(flops=10**8, bytes_accessed=6 * 2**20, transcendentals=10**6),
+        name="ssm_out",
+    )(mixed, ssm_read, ld_cols, enter, ssm_gate, gain_rows)
+
+    heads_own = group // HEAD_SIZE
+    rows = 4 * half
+    stat_shape = jax.ShapeDtypeStruct((2, heads_own, 8, rows), F32)
+    acc_shape = jax.ShapeDtypeStruct((2, heads_own, HEAD_SIZE, rows), F32)
+    params = pltpu.CompilerParams(vmem_limit_bytes=40 * 2**20)
+    cost = pl.CostEstimate(flops=2 * 10**9, bytes_accessed=8 * 2**20, transcendentals=2 * 10**6)
+    smem = pl.BlockSpec(memory_space=pltpu.SMEM)
+    anywhere = pl.BlockSpec(memory_space=pl.ANY)
+    after_local = [st_other]
+    stat, acc = pl.pallas_call(
+        attn_local_kernel,
+        in_specs=[smem] + [VMEM_SPEC] * 2 + [anywhere] * len(after_local),
+        out_specs=[VMEM_SPEC] * 2,
+        out_shape=[stat_shape, acc_shape],
+        compiler_params=params,
+        cost_estimate=cost,
+        name="attn_local",
+    )(jnp.stack([y, core]).astype(jnp.int32), q_own, kv_own, *after_local)
+    after_turn = {1: [cp_other], 2: [], 3: []}
+    for turn in range(1, planes):
+        last = turn == planes - 1
+        later = (z < turn).astype(jnp.int32).reshape(1)
+        outs = [stat_shape, acc_shape]
+        if last:
+            outs = [jax.ShapeDtypeStruct(q_own.shape, F32)] + outs
+        after = after_turn.get(turn, [])
+        *result, stat, acc = pl.pallas_call(
+            functools.partial(attn_remote_kernel, last),
+            in_specs=[smem] + [VMEM_SPEC] * 4 + [anywhere] * len(after),
+            out_specs=[VMEM_SPEC] * len(outs),
+            out_shape=outs,
+            compiler_params=params,
+            cost_estimate=cost,
+            name="attn_remote",
+        )(later, q_own, kv_from[turn - 1], stat, acc, *after)
+    heads_plane = result[0].astype(BF16)
+
+    mine, other = heads_plane[0], send(heads_plane[1], to_y)
+    chip = send(jnp.stack([mine[1], other[1]]), to_core)
+    attn_heads = in_order(
+        in_order(mine[0], other[0], y, axis=1), in_order(chip[0], chip[1], y, axis=1), core, axis=1
+    )
+
+    head_terms = jnp.dot(attn_heads, out_weight, preferred_element_type=F32)
+    out_cols = out_weight.shape[1] // 2
+    away = part(head_terms, 1 - tp_index, out_cols, 1).astype(BF16)
+    came = lax.ppermute(away, "tp", [(0, 1), (1, 0)])
+    attn_mixed = part(head_terms, tp_index, out_cols, 1) + came.astype(F32)
+    return attn_mixed, ssm_output
 
 
 def solution(mesh):
@@ -258,8 +666,16 @@
         P("tp"),
         P("tp", None),
     )
+
+    def program(*arrays):
+        kv_dev, groups_dev = arrays[1].shape[1] // HEAD_SIZE, arrays[5].shape[1] // NS
+        can_split = kv_dev == 4 and groups_dev == 4 and lax.axis_size("tp") == 2
+        if can_split and lax.axis_size("ctx") % 4 == 0 and lax.axis_size("ctx") >= 8:
+            return split_body(*arrays)
+        return body(*arrays)
+
     return jax.shard_map(
-        body,
+        program,
         mesh=mesh,
         in_specs=placed,
         out_specs=(P("ctx", "tp"), P("ctx", "tp")),

time: 509 us -> 148 us (0.29)
  the two profiles are of different devices: /device:TPU:0 before, /device:TPU:24 now
where the time goes in v1:
time: 148 us
  waiting for transfers between devices  52.3 us (35%)
  Pallas kernels  45.3 us (31%)
  starting transfers between devices  18.5 us (12%)
  local copies, waits for them, and re-layouts  15.9 us (11%)
  other arithmetic  12.3 us (8%)
  matrix products  2.42 us (2%)
    ppermute x16, waiting for transfers between devices, send(): return lax.ppermute(x, 'ctx', pairs)  48.6 us
    pallas_call x3, Pallas kernels, split_body(): pl.pallas_call(functools.partial(attn_remote_kernel, last), in_specs=[sme...  21.2 us
    ppermute x16, starting transfers between devices, send(): return lax.ppermute(x, 'ctx', pairs)  16.9 us
    pallas_call x1, Pallas kernels, split_body(): pl.pallas_call(attn_local_kernel, in_specs=[smem] + [VMEM_SPEC] * 2 + [an...  10.7 us
    unnamed x28, local copies, waits for them, and re-layouts  8.88 us
    pallas_call x1, Pallas kernels, split_body(): pl.pallas_call(ssm_local_kernel, grid=(2, groups), in_specs=[wide, narrow...  7.5 us
    pallas_call x1, Pallas kernels, split_body(): pl.pallas_call(ssm_out_kernel, grid=(2, groups), in_specs=[wide, narrow,...  5.92 us
    ppermute x1, waiting for transfers between devices, split_body(): came = lax.ppermute(away, 'tp', [(0, 1), (1, 0)])  3.65 us
  transfers between devices with their start and end apart: 17, of which 6 were waited for; matrix products, arithmetic and copies ran while one was open for 11% of the time, Pallas kernels for 26%

profile of v1, /device:TPU:24, one launch (start us, length us, event | category | flops | bytes accessed | tf_op | source)
XLA Modules:
  0.0 147.8 jit_solution(15420588506042467750)
XLA Ops:
  0.7 1.0 copy.16
  1.7 1.0 copy.15
  2.6 0.7 broadcast_in_dim.107
  3.5 1.2 copy-done.2
  4.8 0.9 copy-done.5
  5.7 0.8 copy-done.6
  6.5 7.5 %ssm_local.1 = (f32[256,2048]{1,0:T(8,128)S(1)}, f32[2,136,2048]{2,1,0:T(8,128)S(1)}) custom-call(bf16[256,2048]{1,0:T(8,128)(2,1)S(1)} %copy-done.2, bf16[256,512]{1,0:T(8,128)(2,1)S(1)} %copy-done.5, bf16[256,512]{1,0:T(8,128)(2,1)S(1)} %copy-done.4, f32[4,256,8]{2,1,0:T(8,128)S(1)} %bitcast.178, f32[4,256,8]{2,1,0:T(8,128)S(1)} %bitcast.176, ...), custom_call_target="tpu_custom_call" | custom-call | flops 400000000 | bytes 6291456 | tf_op jit(solution)/shard_map/ssm_local/pallas_call | solution.py:508
  14.0 1.3 copy-done
  15.3 1.1 constant_dynamic-slice_fusion
  16.5 0.8 dynamic-slice_bitcast_fusion.8
  17.3 0.7 pad_maximum_fusion.10
  18.0 0.4 collective-permute-start.2
  18.4 2.1 %constant_dynamic-slice_fusion.1 = (bf16[256,1024]{1,0:T(8,128)(2,1)}, bf16[1,256,1024]{2,1,0:T(8,128)(2,1)S(1)}) fusion(bf16[256,2048]{1,0:T(8,128)(2,1)} %param.12, s32[]{:T(128)S(6)} %select_n.348, s32[]{:T(128)S(6)} %select_n.347), kind=kLoop, calls=%fused_computation.133 | loop fusion | bytes 2097160 | tf_op jit(solution)/shard_map/dynamic_slice | solution.py:474
  20.6 1.0 maximum_bitcast_fusion.2
  21.6 1.9 %fusion.23 = (bf16[1,2,2,256,128]{4,3,2,1,0:T(8,128)(2,1)}, bf16[2,2,256,128]{3,2,1,0:T(8,128)(2,1)}) fusion(s32[]{:T(128)S(6)} %select_n.353, bf16[2,1,256,256]{3,2,1,0:T(8,128)(2,1)S(1)} %maximum_bitcast_fusion.2, bf16[2,1,256,256]{3,2,1,0:T(8,128)(2,1)} %bitcast.10, s32[]{:T(128)S(6)} %select_n.354), kind=kLoop, calls=%fused_computation.74 | loop fusion | flops 1048576 | bytes 1048584 | tf_op jit(solution)/shard_map/stack | solution.py:485
  23.4 1.5 %collective-permute-start.3 = (bf16[2,2,256,128]{3,2,1,0:T(8,128)(2,1)}, bf16[2,2,256,128]{3,2,1,0:T(8,128)(2,1)}, u32[]{:S(2)}, u32[]{:S(2)}) collective-permute-start(bf16[2,2,256,128]{3,2,1,0:T(8,128)(2,1)} %get-tuple-element.68), channel_id=1, source_target_pairs={{0,4},{2,6},{4,0},{6,2},{8,12},{10,14},{12,8},{14,10},{16,20},{18,... | collective-permute-start | bytes 786440 | tf_op jit(solution)/shard_map/ppermute | solution.py:471
  25.0 7.3 %collective-permute-done.3 = bf16[2,2,256,128]{3,2,1,0:T(8,128)(2,1)} collective-permute-done((bf16[2,2,256,128]{3,2,1,0:T(8,128)(2,1)}, bf16[2,2,256,128]{3,2,1,0:T(8,128)(2,1)}, u32[]{:S(2)}, u32[]{:S(2)}) %collective-permute-start.3) | collective-permute-done | bytes 262176 | tf_op jit(solution)/shard_map/ppermute | solution.py:471
  32.4 1.1 pad_maximum_fusion.3.kv_ref
  33.5 1.9 %collective-permute-start.5 = (bf16[2,2,2,256,128]{4,3,2,1,0:T(8,128)(2,1)S(1)}, bf16[2,2,2,256,128]{4,3,2,1,0:T(8,128)(2,1)S(1)}, u32[]{:S(2)}, u32[]{:S(2)}) collective-permute-start(bf16[2,2,2,256,128]{4,3,2,1,0:T(8,128)(2,1)S(1)} %pad_maximum_fusion.3.kv_ref), channel_id=1, source_target_pairs={{0,16},{2,18},{4,20},{6,22},{8,24},{10,26},{12,28},{14,30},{16,0},... | collective-permute-start | bytes 1572872 | tf_op jit(solution)/shard_map/ppermute | solution.py:471
  35.4 0.4 collective-permute-start.4
  35.9 1.1 fusion.6
  37.0 1.6 %collective-permute-start.1 = (bf16[2,256,512]{2,1,0:T(8,128)(2,1)S(1)}, bf16[2,256,512]{2,1,0:T(8,128)(2,1)S(1)}, u32[]{:S(2)}, u32[]{:S(2)}) collective-permute-start(bf16[2,256,512]{2,1,0:T(8,128)(2,1)S(1)} %get-tuple-element.56), channel_id=1, source_target_pairs={{0,4},{2,6},{4,0},{6,2},{8,12},{10,14},{12,8},{14,10},{16,20},{18,... | collective-permute-start | bytes 1572872 | tf_op jit(solution)/shard_map/ppermute | solution.py:471
  38.6 1.5 %dynamic-slice_select_fusion.1 = (f32[2,136,1024]{2,1,0:T(8,128)S(1)}, f32[2,136,1024]{2,1,0:T(8,128)S(1)}) fusion(f32[2,136,1024]{2,1,0:T(8,128)} %collective-permute-done.7.rest_0_, f32[2,136,2048]{2,1,0:T(8,128)S(1)} %get-tuple-element.11, s32[]{:T(128)S(6)} %select_n.347, pred[]{:T(512)S(6)} %eq.90), kind=kLoop, calls=%fused_computation.14 | loop fusion | flops 557056 | bytes 4456453 | tf_op jit(solution)/shard_map/jit(_where)/select_n | solution.py:532
  40.6 0.6 collective-permute-start.8
  41.1 10.8 %collective-permute-done.1 = bf16[2,256,512]{2,1,0:T(8,128)(2,1)S(1)} collective-permute-done((bf16[2,256,512]{2,1,0:T(8,128)(2,1)S(1)}, bf16[2,256,512]{2,1,0:T(8,128)(2,1)S(1)}, u32[]{:S(2)}, u32[]{:S(2)}) %collective-permute-start.1) | collective-permute-done | bytes 524320 | tf_op jit(solution)/shard_map/ppermute | solution.py:471
  52.0 10.7 %attn_local.1 = (f32[2,4,8,512]{3,2,1,0:T(8,128)S(1)}, f32[2,4,128,512]{3,2,1,0:T(8,128)S(1)}) custom-call(s32[2]{0:T(128)S(1)} %pad_add_fusion.place_ref, bf16[2,2,256,512]{3,2,1,0:T(8,128)(2,1)S(1)} %pad_maximum_fusion.1.q_ref, bf16[2,2,2,256,128]{4,3,2,1,0:T(8,128)(2,1)S(1)} %pad_maximum_fusion.3.kv_ref, f32[2,136,1024]{2,1,0:T(8,128)} %collective-permute-done.7.rest_0_), custom_call_target="tpu_custom_call" | custom-call | flops 2000000000 | bytes 8388608 | tf_op jit(solution)/shard_map/attn_local/pallas_call | solution.py:612
  63.3 3.4 %collective-permute-start.12 = (bf16[2,144,512]{2,1,0:T(8,128)(2,1)S(1)}, bf16[2,144,512]{2,1,0:T(8,128)(2,1)S(1)}, u32[]{:S(2)}, u32[]{:S(2)}) collective-permute-start(bf16[2,144,512]{2,1,0:T(8,128)(2,1)S(1)} %get-tuple-element.70), channel_id=1, source_target_pairs={{0,8},{2,10},{4,12},{6,14},{8,16},{10,18},{12,20},{14,22},{16,24},... | collective-permute-start | bytes 884744 | tf_op jit(solution)/shard_map/ppermute | solution.py:471
  66.7 4.6 %collective-permute-start.14 = (bf16[2,144,512]{2,1,0:T(8,128)(2,1)S(1)}, bf16[2,144,512]{2,1,0:T(8,128)(2,1)S(1)}, u32[]{:S(2)}, u32[]{:S(2)}) collective-permute-start(bf16[2,144,512]{2,1,0:T(8,128)(2,1)S(1)} %get-tuple-element.70), channel_id=1, source_target_pairs={{0,24},{2,26},{4,28},{6,30},{8,0},{10,2},{12,4},{14,6},{16,8},{18,... | collective-permute-start | bytes 884744 | tf_op jit(solution)/shard_map/ppermute | solution.py:471
  71.3 6.5 %attn_remote.3 = (f32[2,4,8,512]{3,2,1,0:T(8,128)S(1)}, f32[2,4,128,512]{3,2,1,0:T(8,128)S(1)}) custom-call(s32[1]{0:T(128)} %bitcast.14.later_ref, bf16[2,2,256,512]{3,2,1,0:T(8,128)(2,1)S(1)} %pad_maximum_fusion.1.q_ref, bf16[2,2,2,256,128]{4,3,2,1,0:T(8,128)(2,1)S(1)} %collective-permute-done.6.kv_ref, f32[2,4,8,512]{3,2,1,0:T(8,128)S(1)} %get-tuple-element.12.stat_in, ...), custom_call_target="tpu_custom_call" | custom-call | flops 2000000000 | bytes 8388608 | tf_op jit(solution)/shard_map/attn_remote/pallas_call | solution.py:629
  77.9 16.8 %collective-permute-done.5.kv_ref = bf16[2,2,2,256,128]{4,3,2,1,0:T(8,128)(2,1)S(1)} collective-permute-done((bf16[2,2,2,256,128]{4,3,2,1,0:T(8,128)(2,1)S(1)}, bf16[2,2,2,256,128]{4,3,2,1,0:T(8,128)(2,1)S(1)}, u32[]{:S(2)}, u32[]{:S(2)}) %collective-permute-start.5) | collective-permute-done | bytes 524320 | tf_op jit(solution)/shard_map/ppermute | solution.py:471
  94.6 6.5 %attn_remote.4 = (f32[2,4,8,512]{3,2,1,0:T(8,128)S(1)}, f32[2,4,128,512]{3,2,1,0:T(8,128)S(1)}) custom-call(s32[1]{0:T(128)} %bitcast.13.later_ref, bf16[2,2,256,512]{3,2,1,0:T(8,128)(2,1)S(1)} %pad_maximum_fusion.1.q_ref, bf16[2,2,2,256,128]{4,3,2,1,0:T(8,128)(2,1)S(1)} %collective-permute-done.5.kv_ref, f32[2,4,8,512]{3,2,1,0:T(8,128)S(1)} %get-tuple-element.14.stat_in, ...), custom_call_target="tpu_custom_call" | custom-call | flops 2000000000 | bytes 8388608 | tf_op jit(solution)/shard_map/attn_remote/pallas_call | solution.py:629
  101.2 8.1 %attn_remote.5 = (f32[2,2,256,512]{3,2,1,0:T(8,128)S(1)}, f32[2,4,8,512]{3,2,1,0:T(8,128)}, f32[2,4,128,512]{3,2,1,0:T(8,128)}) custom-call(s32[1]{0:T(128)} %bitcast.later_ref, bf16[2,2,256,512]{3,2,1,0:T(8,128)(2,1)S(1)} %pad_maximum_fusion.1.q_ref, bf16[2,2,2,256,128]{4,3,2,1,0:T(8,128)(2,1)S(1)} %collective-permute-done.4.kv_ref, ...), custom_call_target="tpu_custom_call" | custom-call | flops 2000000000 | bytes 8388608 | tf_op jit(solution)/shard_map/attn_remote/pallas_call | solution.py:629
  109.5 1.6 %collective-permute-start.9 = (bf16[2,256,512]{2,1,0:T(8,128)(2,1)S(1)}, bf16[2,256,512]{2,1,0:T(8,128)(2,1)S(1)}, u32[]{:S(2)}, u32[]{:S(2)}) collective-permute-start(bf16[2,256,512]{2,1,0:T(8,128)(2,1)S(1)} %slice_bitcast_fusion), channel_id=1, source_target_pairs={{0,4},{2,6},{4,0},{6,2},{8,12},{10,14},{12,8},{14,10},{16,20},{18,... | collective-permute-start | bytes 1572872 | tf_op jit(solution)/shard_map/ppermute | solution.py:471
  111.6 0.3 fusion.20
  111.9 0.6 collective-permute-start.15
  112.5 11.1 %collective-permute-done.9 = bf16[2,256,512]{2,1,0:T(8,128)(2,1)S(1)} collective-permute-done((bf16[2,256,512]{2,1,0:T(8,128)(2,1)S(1)}, bf16[2,256,512]{2,1,0:T(8,128)(2,1)S(1)}, u32[]{:S(2)}, u32[]{:S(2)}) %collective-permute-start.9) | collective-permute-done | bytes 524320 | tf_op jit(solution)/shard_map/ppermute | solution.py:471
  123.8 2.6 %collective-permute-done.15 = bf16[2,128,512]{2,1,0:T(8,128)(2,1)S(1)} collective-permute-done((bf16[2,128,512]{2,1,0:T(8,128)(2,1)S(1)}, bf16[2,128,512]{2,1,0:T(8,128)(2,1)S(1)}, u32[]{:S(2)}, u32[]{:S(2)}) %collective-permute-start.15) | collective-permute-done | bytes 262176 | tf_op jit(solution)/shard_map/ppermute | solution.py:471
  126.6 0.2 add_convert_fusion.1
  127.1 0.2 broadcast_select_fusion.5
  127.3 1.4 slice-done.1
  128.7 2.4 %fusion = f32[256,2048]{1,0:T(8,128)S(1)} fusion(bf16[2048,2048]{1,0:T(8,128)(2,1)S(1)} %bitcast.194, bf16[256,1024]{1,0:T(8,128)(2,1)S(1)} %get-tuple-element.54, bf16[256,1024]{1,0:T(8,128)(2,1)S(1)} %get-tuple-element.53), kind=kOutput, calls=%fused_computation.6 | convolution fusion | flops 2149580800 | bytes 11534336 | tf_op jit(solution)/shard_map/dot_general | solution.py:646
  131.2 1.3 copy-done.8
  132.6 1.6 %collective-permute-start.11 = (bf16[256,1024]{1,0:T(8,128)(2,1)S(1)}, bf16[256,1024]{1,0:T(8,128)(2,1)}, u32[]{:S(2)}, u32[]{:S(2)}) collective-permute-start(bf16[256,1024]{1,0:T(8,128)(2,1)S(1)} %dynamic-slice_convert_fusion), channel_id=1, source_target_pairs={{0,1},{1,0},{2,3},{3,2},{4,5},{5,4},{6,7},{7,6},{8,9},{9,8},{10,11... | collective-permute-start | bytes 1572872 | tf_op jit(solution)/shard_map/ppermute | solution.py:649
  134.4 1.0 copy-done.3
  135.4 0.7 copy-done.1
  136.1 5.9 %ssm_out.1 = f32[256,2048]{1,0:T(8,128)} custom-call(f32[256,2048]{1,0:T(8,128)S(1)} %copy-done.1, bf16[256,512]{1,0:T(8,128)(2,1)S(1)} %copy-done.4, f32[4,256,8]{2,1,0:T(8,128)S(1)} %bitcast.177, bf16[2,128,2048]{2,1,0:T(8,128)(2,1)S(1)} %pad_maximum_fusion.2.enter_ref, bf16[256,2048]{1,0:T(8,128)(2,1)S(1)} %copy-done.3, f32[4,1,512]{2,1,0:T(1,128)S(1)} %bitcast.181), custom_call_target="tpu_custom_call" | custom-call | flops 100000000 | bytes 6291456 | tf_op jit(solution)/shard_map/ssm_out/pallas_call | solution.py:585
  142.0 3.6 %collective-permute-done.11 = bf16[256,1024]{1,0:T(8,128)(2,1)} collective-permute-done((bf16[256,1024]{1,0:T(8,128)(2,1)S(1)}, bf16[256,1024]{1,0:T(8,128)(2,1)}, u32[]{:S(2)}, u32[]{:S(2)}) %collective-permute-start.11) | collective-permute-done | bytes 524320 | tf_op jit(solution)/shard_map/ppermute | solution.py:649
  145.7 2.2 %convert_add_fusion = f32[256,1024]{1,0:T(8,128)} fusion(bf16[256,1024]{1,0:T(8,128)(2,1)} %collective-permute-done.11, f32[256,2048]{1,0:T(8,128)S(1)} %copy-done.9, s32[]{:T(128)S(6)} %select_n.373), kind=kLoop, calls=%fused_computation.11 | loop fusion | flops 524288 | bytes 2621444 | tf_op jit(solution)/shard_map/add | solution.py:650
  (91 shorter events, 3.1 us)
Async XLA Ops:
  0.6 2.9 %copy-start.4 = (bf16[256,512]{1,0:T(8,128)(2,1)S(1)}, bf16[256,512]{1,0:T(8,128)(2,1)}, u32[]{:S(2)}) copy-start(bf16[256,512]{1,0:T(8,128)(2,1)} %read_ref.3) | copy-start | bytes 786436
  3.5 1.2 copy-start.2
  4.8 0.9 copy-start.5
  5.7 0.8 copy-start.6
  14.0 1.4 copy-start
  15.3 1.1 copy-start.10
  15.3 1.2 copy-start.11
  16.4 22.2 %collective-permute-start.7 = (f32[2,136,1024]{2,1,0:T(8,128)}, f32[2,136,1024]{2,1,0:T(8,128)}, u32[]{:S(2)}, u32[]{:S(2)}) collective-permute-start(f32[2,136,1024]{2,1,0:T(8,128)} %constant_dynamic-slice_fusion), channel_id=1, source_target_pairs={{0,2},{2,0},{4,6},{6,4},{8,10},{10,8},{12,14},{14,12},{16,18},{18,... | collective-permute-start | bytes 3342344 | tf_op jit(solution)/shard_map/ppermute | solution.py:471
  18.0 3.6 %collective-permute-start.2 = (bf16[2,256,256]{2,1,0:T(8,128)(2,1)}, bf16[2,256,256]{2,1,0:T(8,128)(2,1)}, u32[]{:S(2)}, u32[]{:S(2)}) collective-permute-start(bf16[2,256,256]{2,1,0:T(8,128)(2,1)} %pad_maximum_fusion.10), channel_id=1, source_target_pairs={{0,2},{2,0},{4,6},{6,4},{8,10},{10,8},{12,14},{14,12},{16,18},{18,... | collective-permute-start | bytes 786440 | tf_op jit(solution)/shard_map/ppermute | solution.py:471
  20.5 15.4 %collective-permute-start = (bf16[256,1024]{1,0:T(8,128)(2,1)}, bf16[256,1024]{1,0:T(8,128)(2,1)}, u32[]{:S(2)}, u32[]{:S(2)}) collective-permute-start(bf16[256,1024]{1,0:T(8,128)(2,1)} %get-tuple-element.57), channel_id=1, source_target_pairs={{0,2},{2,0},{4,6},{6,4},{8,10},{10,8},{12,14},{14,12},{16,18},{18,... | collective-permute-start | bytes 1572872 | tf_op jit(solution)/shard_map/ppermute | solution.py:471
  23.4 9.0 %collective-permute-start.3 = (bf16[2,2,256,128]{3,2,1,0:T(8,128)(2,1)}, bf16[2,2,256,128]{3,2,1,0:T(8,128)(2,1)}, u32[]{:S(2)}, u32[]{:S(2)}) collective-permute-start(bf16[2,2,256,128]{3,2,1,0:T(8,128)(2,1)} %get-tuple-element.68), channel_id=1, source_target_pairs={{0,4},{2,6},{4,0},{6,2},{8,12},{10,14},{12,8},{14,10},{16,20},{18,... | collective-permute-start | bytes 786440 | tf_op jit(solution)/shard_map/ppermute | solution.py:471
  33.5 33.3 %collective-permute-start.6 = (bf16[2,2,2,256,128]{4,3,2,1,0:T(8,128)(2,1)S(1)}, bf16[2,2,2,256,128]{4,3,2,1,0:T(8,128)(2,1)S(1)}, u32[]{:S(2)}, u32[]{:S(2)}) collective-permute-start(bf16[2,2,2,256,128]{4,3,2,1,0:T(8,128)(2,1)S(1)} %pad_maximum_fusion.3.kv_ref), channel_id=1, source_target_pairs={{0,8},{2,10},{4,12},{6,14},{8,16},{10,18},{12,20},{14,22},{16,24},... | collective-permute-start | bytes 1572872 | tf_op jit(solution)/shard_map/ppermute | solution.py:471
  33.5 61.1 %collective-permute-start.5 = (bf16[2,2,2,256,128]{4,3,2,1,0:T(8,128)(2,1)S(1)}, bf16[2,2,2,256,128]{4,3,2,1,0:T(8,128)(2,1)S(1)}, u32[]{:S(2)}, u32[]{:S(2)}) collective-permute-start(bf16[2,2,2,256,128]{4,3,2,1,0:T(8,128)(2,1)S(1)} %pad_maximum_fusion.3.kv_ref), channel_id=1, source_target_pairs={{0,16},{2,18},{4,20},{6,22},{8,24},{10,26},{12,28},{14,30},{16,0},... | collective-permute-start | bytes 1572872 | tf_op jit(solution)/shard_map/ppermute | solution.py:471
  35.4 65.8 %collective-permute-start.4 = (bf16[2,2,2,256,128]{4,3,2,1,0:T(8,128)(2,1)S(1)}, bf16[2,2,2,256,128]{4,3,2,1,0:T(8,128)(2,1)S(1)}, u32[]{:S(2)}, u32[]{:S(2)}) collective-permute-start(bf16[2,2,2,256,128]{4,3,2,1,0:T(8,128)(2,1)S(1)} %pad_maximum_fusion.3.kv_ref), channel_id=1, source_target_pairs={{0,24},{2,26},{4,28},{6,30},{8,0},{10,2},{12,4},{14,6},{16,8},{18,... | collective-permute-start | bytes 1572872 | tf_op jit(solution)/shard_map/ppermute | solution.py:471
  37.0 14.9 %collective-permute-start.1 = (bf16[2,256,512]{2,1,0:T(8,128)(2,1)S(1)}, bf16[2,256,512]{2,1,0:T(8,128)(2,1)S(1)}, u32[]{:S(2)}, u32[]{:S(2)}) collective-permute-start(bf16[2,256,512]{2,1,0:T(8,128)(2,1)S(1)} %get-tuple-element.56), channel_id=1, source_target_pairs={{0,4},{2,6},{4,0},{6,2},{8,12},{10,14},{12,8},{14,10},{16,20},{18,... | collective-permute-start | bytes 1572872 | tf_op jit(solution)/shard_map/ppermute | solution.py:471
  40.6 22.2 %collective-permute-start.8 = (bf16[2,144,512]{2,1,0:T(8,128)(2,1)S(1)}, bf16[2,144,512]{2,1,0:T(8,128)(2,1)S(1)}, u32[]{:S(2)}, u32[]{:S(2)}) collective-permute-start(bf16[2,144,512]{2,1,0:T(8,128)(2,1)S(1)} %fusion.12), channel_id=1, source_target_pairs={{0,4},{2,6},{4,0},{6,2},{8,12},{10,14},{12,8},{14,10},{16,20},{18,... | collective-permute-start | bytes 884744 | tf_op jit(solution)/shard_map/ppermute | solution.py:471
  63.3 47.8 %collective-permute-start.12 = (bf16[2,144,512]{2,1,0:T(8,128)(2,1)S(1)}, bf16[2,144,512]{2,1,0:T(8,128)(2,1)S(1)}, u32[]{:S(2)}, u32[]{:S(2)}) collective-permute-start(bf16[2,144,512]{2,1,0:T(8,128)(2,1)S(1)} %get-tuple-element.70), channel_id=1, source_target_pairs={{0,8},{2,10},{4,12},{6,14},{8,16},{10,18},{12,20},{14,22},{16,24},... | collective-permute-start | bytes 884744 | tf_op jit(solution)/shard_map/ppermute | solution.py:471
  66.7 44.4 %collective-permute-start.13 = (bf16[2,144,512]{2,1,0:T(8,128)(2,1)S(1)}, bf16[2,144,512]{2,1,0:T(8,128)(2,1)S(1)}, u32[]{:S(2)}, u32[]{:S(2)}) collective-permute-start(bf16[2,144,512]{2,1,0:T(8,128)(2,1)S(1)} %get-tuple-element.70), channel_id=1, source_target_pairs={{0,16},{2,18},{4,20},{6,22},{8,24},{10,26},{12,28},{14,30},{16,0},... | collective-permute-start | bytes 884744 | tf_op jit(solution)/shard_map/ppermute | solution.py:471
  66.7 44.4 %collective-permute-start.14 = (bf16[2,144,512]{2,1,0:T(8,128)(2,1)S(1)}, bf16[2,144,512]{2,1,0:T(8,128)(2,1)S(1)}, u32[]{:S(2)}, u32[]{:S(2)}) collective-permute-start(bf16[2,144,512]{2,1,0:T(8,128)(2,1)S(1)} %get-tuple-element.70), channel_id=1, source_target_pairs={{0,24},{2,26},{4,28},{6,30},{8,0},{10,2},{12,4},{14,6},{16,8},{18,... | collective-permute-start | bytes 884744 | tf_op jit(solution)/shard_map/ppermute | solution.py:471
  109.5 14.1 %collective-permute-start.9 = (bf16[2,256,512]{2,1,0:T(8,128)(2,1)S(1)}, bf16[2,256,512]{2,1,0:T(8,128)(2,1)S(1)}, u32[]{:S(2)}, u32[]{:S(2)}) collective-permute-start(bf16[2,256,512]{2,1,0:T(8,128)(2,1)S(1)} %slice_bitcast_fusion), channel_id=1, source_target_pairs={{0,4},{2,6},{4,0},{6,2},{8,12},{10,14},{12,8},{14,10},{16,20},{18,... | collective-permute-start | bytes 1572872 | tf_op jit(solution)/shard_map/ppermute | solution.py:471
  111.6 15.7 %slice-start = ((s8[8388608]{0:T(1024)(128)(4,1)}), s8[4194304]{0:T(1024)(128)(4,1)S(1)}, s32[]{:S(2)}) async-start(s8[8388608]{0:T(1024)(128)(4,1)} %bitcast.193), calls=%async_computation | async-start | bytes 8388608
  111.9 14.5 %collective-permute-start.15 = (bf16[2,128,512]{2,1,0:T(8,128)(2,1)S(1)}, bf16[2,128,512]{2,1,0:T(8,128)(2,1)S(1)}, u32[]{:S(2)}, u32[]{:S(2)}) collective-permute-start(bf16[2,128,512]{2,1,0:T(8,128)(2,1)S(1)} %broadcast_select_fusion.10), channel_id=1, source_target_pairs={{0,4},{2,6},{4,0},{6,2},{8,12},{10,14},{12,8},{14,10},{16,20},{18,... | collective-permute-start | bytes 786440 | tf_op jit(solution)/shard_map/ppermute | solution.py:471
  123.6 3.4 %collective-permute-start.10 = (bf16[2,256,512]{2,1,0:T(8,128)(2,1)S(1)}, bf16[2,256,512]{2,1,0:T(8,128)(2,1)S(1)}, u32[]{:S(2)}, u32[]{:S(2)}) collective-permute-start(bf16[2,256,512]{2,1,0:T(8,128)(2,1)S(1)} %pad_maximum_fusion.5), channel_id=1, source_target_pairs={{0,2},{2,0},{4,6},{6,4},{8,10},{10,8},{12,14},{14,12},{16,18},{18,... | collective-permute-start | bytes 1572872 | tf_op jit(solution)/shard_map/ppermute | solution.py:471
  126.5 2.2 %slice-start.1 = ((s8[8388608]{0:T(1024)(128)(4,1)}), s8[4194304]{0:T(1024)(128)(4,1)S(1)}, s32[]{:S(2)}) async-start(s8[8388608]{0:T(1024)(128)(4,1)} %bitcast.193), calls=%async_computation.1 | async-start | bytes 8388608
  127.0 7.2 %collective-permute-start.16 = (bf16[2,128,1024]{2,1,0:T(8,128)(2,1)S(1)}, bf16[2,128,1024]{2,1,0:T(8,128)(2,1)S(1)}, u32[]{:S(2)}, u32[]{:S(2)}) collective-permute-start(bf16[2,128,1024]{2,1,0:T(8,128)(2,1)S(1)} %broadcast_select_fusion.2), channel_id=1, source_target_pairs={{0,2},{2,0},{4,6},{6,4},{8,10},{10,8},{12,14},{14,12},{16,18},{18,... | collective-permute-start | bytes 1572872 | tf_op jit(solution)/shard_map/ppermute | solution.py:471
  131.2 1.3 copy-start.8
  132.6 13.1 %collective-permute-start.11 = (bf16[256,1024]{1,0:T(8,128)(2,1)S(1)}, bf16[256,1024]{1,0:T(8,128)(2,1)}, u32[]{:S(2)}, u32[]{:S(2)}) collective-permute-start(bf16[256,1024]{1,0:T(8,128)(2,1)S(1)} %dynamic-slice_convert_fusion), channel_id=1, source_target_pairs={{0,1},{1,0},{2,3},{3,2},{4,5},{5,4},{6,7},{7,6},{8,9},{9,8},{10,11... | collective-permute-start | bytes 1572872 | tf_op jit(solution)/shard_map/ppermute | solution.py:649
  134.1 1.2 copy-start.3
  134.1 1.2 copy-start.7
  134.3 1.8 %copy-start.1 = (f32[256,2048]{1,0:T(8,128)S(1)}, f32[256,2048]{1,0:T(8,128)}, u32[]{:S(2)}) copy-start(f32[256,2048]{1,0:T(8,128)} %copy-done) | copy-start | bytes 6291460
  136.1 9.6 %copy-start.9 = (f32[256,2048]{1,0:T(8,128)S(1)}, f32[256,2048]{1,0:T(8,128)}, u32[]{:S(2)}) copy-start(f32[256,2048]{1,0:T(8,128)} %copy-done.8) | copy-start | bytes 6291460

commit v2 on v1

--- a/solution.py
+++ b/solution.py
@@ -264,7 +264,7 @@
     return jnp.where(lane < P_SIZE, first, second)
 
 
-def ssm_local_kernel(x_ref, write_ref, read_ref, step_ref, ldc_ref, ldr_ref, skip_ref, mixed_ref, state_ref):
+def ssm_local_kernel(x_ref, write_ref, read_ref, step_ref, ldc_ref, ldr_ref, skip_ref, _, mixed_ref, state_ref):
     span = x_ref.shape[0]
     per_group = step_ref.shape[2]
     row = lax.broadcasted_iota(jnp.int32, (span, span), 0)
@@ -336,19 +336,35 @@
     return m_new, l_new, acc_new
 
 
-def plane_rows(ref, which, half, span):
-    return ref[:, which, :, pl.ds(half * span, span), :].reshape(4 * span, HEAD_SIZE)
-
-
-def query_tile(q_ref, turn, half, head, span):
-    return q_ref[turn, :, pl.ds(half * span, span), pl.ds(head * HEAD_SIZE, HEAD_SIZE)].reshape(2 * span, HEAD_SIZE)
-
-
-def attn_local_kernel(place_ref, q_ref, kv_ref, *rest):
-    stat_ref, acc_ref = rest[-2:]
+def plane_rows(ref, half, which):
+    chunk = ref[:, which] if half is None else ref[half, :, which]
+    return chunk.reshape(-1, HEAD_SIZE)
+
+
+def update_tile(q_refs, half, turn, head, keys, values_t, allowed, stat_ref, acc_ref, first):
+    span = q_refs[0].shape[0] // 2
+    q = jnp.concatenate(
+        [
+            ref[pl.ds(half * span, span), pl.ds(head * HEAD_SIZE, HEAD_SIZE)]
+            for ref in q_refs[2 * turn : 2 * turn + 2]
+        ],
+        axis=0,
+    )
+    where = pl.ds(turn * 2 * span, 2 * span)
+    running = (None, None, None)
+    if not first:
+        running = (stat_ref[head, pl.ds(0, 1), where], stat_ref[head, pl.ds(1, 1), where], acc_ref[head, :, where])
+    running = attend_tile(q, keys, values_t, running, allowed)
+    stat_ref[head, pl.ds(0, 1), where] = running[0]
+    stat_ref[head, pl.ds(1, 1), where] = running[1]
+    acc_ref[head, :, where] = running[2]
+
+
+def attn_local_kernel(place_ref, *refs):
+    q_refs, kv_ref, (stat_ref, acc_ref) = refs[:4], refs[4], refs[-2:]
     y, core = place_ref[0], place_ref[1]
-    span = q_ref.shape[2] // 2
-    heads = q_ref.shape[3] // HEAD_SIZE
+    span = q_refs[0].shape[0] // 2
+    heads = q_refs[0].shape[1] // HEAD_SIZE
     tile = 2 * span
 
     def position(shape, dim, half):
@@ -356,73 +372,47 @@
         block = jnp.where(at < span, core, 1 - core)
         return (block if half == 0 else 1 - block) * span + at % span
 
-    def update(half, turn, head, keys, values_t, allowed, first):
-        where = pl.ds(pl.multiple_of(turn * tile, tile), tile)
-        running = (None, None, None)
-        if not first:
-            running = (
-                stat_ref[half, head, pl.ds(0, 1), where],
-                stat_ref[half, head, pl.ds(1, 1), where],
-                acc_ref[half, head, :, where],
-            )
-        running = attend_tile(query_tile(q_ref, turn, half, head, span), keys, values_t, running, allowed)
-        stat_ref[half, head, pl.ds(0, 1), where] = running[0]
-        stat_ref[half, head, pl.ds(1, 1), where] = running[1]
-        acc_ref[half, head, :, where] = running[2]
-
     for half in range(2):
+        state = stat_ref.at[half], acc_ref.at[half]
         allowed = position((tile, 1), 0, half) <= position((1, tile), 1, half)
+        parts = []
         for turn in range(2):
-            keys = kv_ref[turn, 0, :, pl.ds(half * span, span), :].reshape(tile, HEAD_SIZE)
-            values_t = kv_ref[turn, 1, :, pl.ds(half * span, span), :].reshape(tile, HEAD_SIZE).T
+            keys = kv_ref[half, 2 * turn : 2 * turn + 2, 0].reshape(tile, HEAD_SIZE)
+            values_t = kv_ref[half, 2 * turn : 2 * turn + 2, 1].reshape(tile, HEAD_SIZE).T
+            parts.append((keys, values_t))
             for head in range(heads):
-                update(half, turn, head, keys, values_t, allowed, True)
-        after = 1 - y if half == 0 else y
-        keys = kv_ref[1 - after, 0, :, pl.ds(half * span, span), :].reshape(tile, HEAD_SIZE)
-        values_t = kv_ref[1 - after, 1, :, pl.ds(half * span, span), :].reshape(tile, HEAD_SIZE).T
-        for head in range(heads):
-            update(half, after, head, keys, values_t, None, False)
-    keys, values_t = plane_rows(kv_ref, 0, 0, span), plane_rows(kv_ref, 1, 0, span).T
+                update_tile(q_refs, half, turn, head, keys, values_t, allowed, *state, True)
+        for turn in range(2):
+
+            @pl.when(y == (1 - turn if half == 0 else turn))
+            def _():
+                for head in range(heads):
+                    update_tile(q_refs, half, turn, head, *parts[1 - turn], None, *state, False)
+
+    attn_units(q_refs, 1, kv_ref, 0, stat_ref, acc_ref)
+
+
+def attn_units(q_refs, half, kv_ref, part, stat_ref, acc_ref):
+    keys, values_t = plane_rows(kv_ref, part, 0), plane_rows(kv_ref, part, 1).T
     for turn in range(2):
-        for head in range(heads):
-            update(1, turn, head, keys, values_t, None, False)
-
-
-def attn_remote_kernel(last, later_ref, q_ref, kv_ref, stat_in, acc_in, *rest):
+        for head in range(acc_ref.shape[1]):
+            update_tile(q_refs, half, turn, head, keys, values_t, None, stat_ref.at[half], acc_ref.at[half], False)
+
+
+def attn_remote_kernel(last, later_ref, *refs):
+    q_refs, kv_ref = refs[:4], refs[4]
+    outs = refs[-3:] if last else refs[-2:]
+    stat_ref, acc_ref = outs[-2:]
+    later = later_ref[0]
+    attn_units(q_refs, later, kv_ref, later, stat_ref, acc_ref)
+    attn_units(q_refs, 1, kv_ref, 0, stat_ref, acc_ref)
     if last:
-        out_ref, stat_ref, acc_ref = rest[-3:]
-    else:
-        stat_ref, acc_ref = rest[-2:]
-    later = later_ref[0]
-    span = q_ref.shape[2] // 2
-    heads = q_ref.shape[3] // HEAD_SIZE
-    tile = 2 * span
-    stat_ref[...] = stat_in[...]
-    acc_ref[...] = acc_in[...]
-
-    def unit(half, part):
-        keys, values_t = plane_rows(kv_ref, 0, part, span), plane_rows(kv_ref, 1, part, span).T
-        for turn in range(2):
-            where = pl.ds(turn * tile, tile)
-            for head in range(heads):
-                running = (
-                    stat_ref[half, head, pl.ds(0, 1), where],
-                    stat_ref[half, head, pl.ds(1, 1), where],
-                    acc_ref[half, head, :, where],
-                )
-                running = attend_tile(query_tile(q_ref, turn, half, head, span), keys, values_t, running, None)
-                stat_ref[half, head, pl.ds(0, 1), where] = running[0]
-                stat_ref[half, head, pl.ds(1, 1), where] = running[1]
-                acc_ref[half, head, :, where] = running[2]
-
-    unit(1, 0)
-    unit(later, later)
-    if last:
+        span = q_refs[0].shape[0] // 2
         for half in range(2):
-            for head in range(heads):
+            for head in range(acc_ref.shape[1]):
                 scaled = acc_ref[half, head] / stat_ref[half, head, pl.ds(1, 1), :]
-                out_ref[:, :, pl.ds(half * span, span), pl.ds(head * HEAD_SIZE, HEAD_SIZE)] = scaled.T.reshape(
-                    2, 2, span, HEAD_SIZE
+                outs[0][:, pl.ds(half * span, span), pl.ds(head * HEAD_SIZE, HEAD_SIZE)] = scaled.T.reshape(
+                    4, span, HEAD_SIZE
                 )
 
 
@@ -476,21 +466,27 @@
     def in_order(mine, other, at, axis=0):
         return jnp.concatenate([jnp.where(at == 0, mine, other), jnp.where(at == 0, other, mine)], axis=axis)
 
-    def both(which):
-        return jnp.stack(
-            [part(key_head_array, which, 2 * HEAD_SIZE, 1), part(value_head_array, which, 2 * HEAD_SIZE, 1)]
-        )
-
-    kv_chip = jnp.stack([both(core), send(both(1 - core), to_core)], axis=1)
-    kv_own = jnp.stack(
-        [part(kv_chip, y, HEAD_SIZE, 3), send(part(kv_chip, 1 - y, HEAD_SIZE, 3), to_y)]
-    )
-    kv_from = [
-        send(kv_own, [(i, (i + 4 * turn) % (4 * planes)) for i in everyone]) for turn in range(1, planes)
-    ]
-
-    q_chip = jnp.stack([part(queries, core, 2 * group, 1), send(part(queries, 1 - core, 2 * group, 1), to_core)])
-    q_own = jnp.stack([part(q_chip, y, group, 2), send(part(q_chip, 1 - y, group, 2), to_y)])
+    near = range(4)
+    near_pairs = [None, to_core, to_y, [(i, i ^ 3) for i in everyone]]
+    head_of = [2 * (core if k in (0, 2) else 1 - core) + (y if k < 2 else 1 - y) for k in near]
+
+    def kv_piece(which):
+        cut = [part(x, which, HEAD_SIZE, 1).reshape(2, half, HEAD_SIZE) for x in (key_head_array, value_head_array)]
+        return jnp.stack(cut, axis=1)
+
+    kv_near = {k: send(kv_piece(head_of[k]), near_pairs[k]) for k in (2, 3, 1)}
+    kv_near[0] = kv_piece(head_of[0])
+    kv_own = jnp.stack([kv_near[k] for k in near], axis=1)
+
+    def across(by):
+        return [(i, i ^ (4 * by)) for i in everyone]
+
+    kv_from = {by: send(kv_own, across(by)) for by in range(1, planes)}
+
+    q_mine, q_sent = part(queries, core, 2 * group, 1), part(queries, 1 - core, 2 * group, 1)
+    q_other = send(q_sent, to_core)
+    q_far = send(jnp.stack([part(q_mine, 1 - y, group, 1), part(q_other, 1 - y, group, 1)]), to_y)
+    q_near = [part(q_mine, y, group, 1), part(q_other, y, group, 1), q_far[0], q_far[1]]
 
     groups = ssm_write.shape[1] // NS
     per_group = step_size.shape[0] // groups
@@ -516,6 +512,7 @@
             columns,
             pl.BlockSpec((1, per_group, half), lambda b, g: (g, 0, b)),
             per_row,
+            pl.BlockSpec(memory_space=pl.ANY),
         ],
         out_specs=[wide, pl.BlockSpec((1, NS + 8, width), lambda b, g: (b, 0, g))],
         out_shape=[
@@ -525,7 +522,7 @@
         compiler_params=pltpu.CompilerParams(vmem_limit_bytes=32 * 2**20),
         cost_estimate=pl.CostEstimate(flops=4 * 10**8, bytes_accessed=6 * 2**20, transcendentals=10**6),
         name="ssm_local",
-    )(ssm_input, ssm_write, ssm_read, step_cols, ld_cols, ld_rows, skip_rows)
+    )(ssm_input, ssm_write, ssm_read, step_cols, ld_cols, ld_rows, skip_rows, kv_near[1][0, 0, :16])
 
     st_mine = part(states, core, 2 * width, 2)
     st_other = send(part(states, 1 - core, 2 * width, 2), to_core)
@@ -542,24 +539,26 @@
     cp_zero, cp_one = jnp.where(y == 0, cp_mine, cp_other), jnp.where(y == 0, cp_other, cp_mine)
     early_plane = chain(unpack(cp_zero[0]), unpack(cp_one[0]))
     late_plane = chain(unpack(cp_one[1]), unpack(cp_zero[1]))
-    plane_pack = jnp.stack([pack(*early_plane), pack(*late_plane)])
-    plane_from = jnp.stack(
-        [plane_pack]
-        + [send(plane_pack, [(i, (i + 4 * turn) % (4 * planes)) for i in everyone]) for turn in range(1, planes)]
-    )
-
-    def of_plane(at):
-        return lax.dynamic_index_in_dim(plane_from, (z - at) % planes, 0, keepdims=False)
-
-    total = (jnp.zeros((NS, width), F32), jnp.zeros((1, width), F32))
-    enter_early = total[0]
-    for at in range(planes):
-        enter_early = jnp.where(z == at, total[0], enter_early)
-        total = chain(total, unpack(of_plane(at)[0]))
-    enter_late = total[0]
-    for at in range(planes - 1, -1, -1):
-        enter_late = jnp.where(z == at, total[0], enter_late)
-        total = chain(total, unpack(of_plane(at)[1]))
+    def ordered_pair(mine, other, low):
+        first = jax.tree.map(lambda a, b: jnp.where(low, a, b), mine, other)
+        second = jax.tree.map(lambda a, b: jnp.where(low, b, a), mine, other)
+        return chain(first[0], second[0]), chain(second[1], first[1])
+
+    zero = (jnp.zeros((NS, width), F32), jnp.zeros((1, width), F32))
+    span_own = (early_plane, late_plane)
+    before, after = zero, zero
+    z_came = []
+    for bit in range(planes.bit_length() - 1):
+        low = (z >> bit) % 2 == 0
+        span_pack = jnp.stack([pack(*span_own[0]), pack(*span_own[1])])
+        came = send(span_pack, across(1 << bit))
+        z_came.append(came)
+        span_other = (unpack(came[0]), unpack(came[1]))
+        before = jax.tree.map(lambda a, b: jnp.where(low, b, a), chain(span_other[0], before), before)
+        after = jax.tree.map(lambda a, b: jnp.where(low, a, b), chain(span_other[1], after), after)
+        span_own = ordered_pair(span_own, span_other, low)
+    enter_early = before[0]
+    enter_late = chain(span_own[0], after)[0]
 
     def step_on(state, packed):
         block = unpack(packed)
@@ -602,47 +601,45 @@
 
     heads_own = group // HEAD_SIZE
     rows = 4 * half
-    stat_shape = jax.ShapeDtypeStruct((2, heads_own, 8, rows), F32)
-    acc_shape = jax.ShapeDtypeStruct((2, heads_own, HEAD_SIZE, rows), F32)
-    params = pltpu.CompilerParams(vmem_limit_bytes=40 * 2**20)
+    state_shapes = [
+        jax.ShapeDtypeStruct((2, heads_own, 8, rows), F32),
+        jax.ShapeDtypeStruct((2, heads_own, HEAD_SIZE, rows), F32),
+    ]
+    out_shape = jax.ShapeDtypeStruct((4, tok_dev, group), F32)
+    params = pltpu.CompilerParams(vmem_limit_bytes=28 * 2**20)
     cost = pl.CostEstimate(flops=2 * 10**9, bytes_accessed=8 * 2**20, transcendentals=2 * 10**6)
     smem = pl.BlockSpec(memory_space=pltpu.SMEM)
     anywhere = pl.BlockSpec(memory_space=pl.ANY)
-    after_local = [st_other]
-    stat, acc = pl.pallas_call(
-        attn_local_kernel,
-        in_specs=[smem] + [VMEM_SPEC] * 2 + [anywhere] * len(after_local),
-        out_specs=[VMEM_SPEC] * 2,
-        out_shape=[stat_shape, acc_shape],
-        compiler_params=params,
-        cost_estimate=cost,
-        name="attn_local",
-    )(jnp.stack([y, core]).astype(jnp.int32), q_own, kv_own, *after_local)
-    after_turn = {1: [cp_other], 2: [], 3: []}
-    for turn in range(1, planes):
-        last = turn == planes - 1
-        later = (z < turn).astype(jnp.int32).reshape(1)
-        outs = [stat_shape, acc_shape]
-        if last:
-            outs = [jax.ShapeDtypeStruct(q_own.shape, F32)] + outs
-        after = after_turn.get(turn, [])
-        *result, stat, acc = pl.pallas_call(
-            functools.partial(attn_remote_kernel, last),
-            in_specs=[smem] + [VMEM_SPEC] * 4 + [anywhere] * len(after),
+
+    def attend(kernel, name, scalars, kv, states, after, last=False):
+        outs = ([out_shape] if last else []) + state_shapes
+        return pl.pallas_call(
+            kernel,
+            in_specs=[smem] + [VMEM_SPEC] * (5 + len(states)) + [anywhere] * len(after),
             out_specs=[VMEM_SPEC] * len(outs),
             out_shape=outs,
+            input_output_aliases={6 + k: len(outs) - 2 + k for k in range(len(states))},
             compiler_params=params,
             cost_estimate=cost,
-            name="attn_remote",
-        )(later, q_own, kv_from[turn - 1], stat, acc, *after)
+            name=name,
+        )(scalars, *q_near, kv, *states, *[x[0, :16, :128] for x in after])
+
+    place = jnp.stack([y, core]).astype(jnp.int32)
+    states = attend(attn_local_kernel, "attn_local", place, kv_own, [], [])
+    for by in range(1, planes):
+        last = by == planes - 1
+        later = (z ^ by > z).astype(jnp.int32).reshape(1)
+        waits = {1: [cp_other], 3: [z_came[0]]}.get(by, [])
+        *result, stat, acc = attend(
+            functools.partial(attn_remote_kernel, last), "attn_remote", later, kv_from[by], states, waits, last
+        )
+        states = [stat, acc]
     heads_plane = result[0].astype(BF16)
 
-    mine, other = heads_plane[0], send(heads_plane[1], to_y)
-    chip = send(jnp.stack([mine[1], other[1]]), to_core)
+    pieces = [heads_plane[0]] + [send(heads_plane[k], near_pairs[k]) for k in (1, 2, 3)]
     attn_heads = in_order(
-        in_order(mine[0], other[0], y, axis=1), in_order(chip[0], chip[1], y, axis=1), core, axis=1
-    )
-
+        in_order(pieces[0], pieces[2], y, axis=1), in_order(pieces[1], pieces[3], y, axis=1), core, axis=1
+    )
     head_terms = jnp.dot(attn_heads, out_weight, preferred_element_type=F32)
     out_cols = out_weight.shape[1] // 2
     away = part(head_terms, 1 - tp_index, out_cols, 1).astype(BF16)
@@ -670,7 +667,7 @@
     def program(*arrays):
         kv_dev, groups_dev = arrays[1].shape[1] // HEAD_SIZE, arrays[5].shape[1] // NS
         can_split = kv_dev == 4 and groups_dev == 4 and lax.axis_size("tp") == 2
-        if can_split and lax.axis_size("ctx") % 4 == 0 and lax.axis_size("ctx") >= 8:
+        if can_split and lax.axis_size("ctx") in (8, 16, 32, 64):
             return split_body(*arrays)
         return body(*arrays)
 

time: 148 us -> 131 us (0.89)
  the two profiles are of different devices: /device:TPU:24 before, /device:TPU:0 now
where the time goes in v2:
time: 131 us
  Pallas kernels  44.7 us (34%)
  waiting for transfers between devices  38.1 us (29%)
  starting transfers between devices  20.4 us (16%)
  local copies, waits for them, and re-layouts  12.3 us (9%)
  other arithmetic  11.2 us (9%)
  matrix products  2.42 us (2%)
  between operations  1.57 us (1%)
    pallas_call x4, Pallas kernels, attend(): pl.pallas_call(kernel, in_specs=[smem] + [VMEM_SPEC] * (5 + len(states))...  31.2 us
    ppermute x17, waiting for transfers between devices, send(): return lax.ppermute(x, 'ctx', pairs)  30.3 us
    ppermute x17, starting transfers between devices, send(): return lax.ppermute(x, 'ctx', pairs)  18.8 us
    ppermute x1, waiting for transfers between devices, split_body(): came = lax.ppermute(away, 'tp', [(0, 1), (1, 0)])  7.75 us
    pallas_call x1, Pallas kernels, split_body(): pl.pallas_call(ssm_local_kernel, grid=(2, groups), in_specs=[wide, narrow...  7.53 us
    pallas_call x1, Pallas kernels, split_body(): pl.pallas_call(ssm_out_kernel, grid=(2, groups), in_specs=[wide, narrow,...  5.92 us
    unnamed x38, local copies, waits for them, and re-layouts  5.57 us
    dynamic_slice x3, local copies, waits for them, and re-layouts, part(): return lax.dynamic_slice_in_dim(x, which * width, width, axis)  3.7 us
  transfers between devices with their start and end apart: 18, of which 8 were waited for; matrix products, arithmetic and copies ran while one was open for 13% of the time, Pallas kernels for 25%

profile of v2, /device:TPU:0, one launch (start us, length us, event | category | flops | bytes accessed | tf_op | source)
XLA Modules:
  0.0 130.6 jit_solution(1374473773212437959)
XLA Ops:
  0.7 1.8 %constant_dynamic-slice_fusion.7 = (bf16[256,128]{1,0:T(8,128)(2,1)}, bf16[256,128]{1,0:T(8,128)(2,1)S(1)}, bf16[256,128]{1,0:T(8,128)(2,1)}, bf16[256,128]{1,0:...) fusion(bf16[256,512]{1,0:T(8,128)(2,1)} %param.14, ...), kind=kLoop, calls=%fused_computation.137 | loop fusion | bytes 1048592 | tf_op jit(solution)/shard_map/dynamic_slice | solution.py:464
  2.5 0.5 collective-permute-start.2
  3.1 0.7 pad_maximum_fusion.12
  3.7 2.5 %collective-permute-start.3 = (bf16[2,2,128,128]{3,2,1,0:T(8,128)(2,1)}, bf16[2,2,128,128]{3,2,1,0:T(8,128)(2,1)}, u32[]{:S(2)}, u32[]{:S(2)}) collective-permute-start(bf16[2,2,128,128]{3,2,1,0:T(8,128)(2,1)} %pad_maximum_fusion.12), channel_id=1, source_target_pairs={{0,4},{2,6},{4,0},{6,2},{8,12},{10,14},{12,8},{14,10},{16,20},{18,... | collective-permute-start | bytes 393224 | tf_op jit(solution)/shard_map/ppermute | solution.py:461
  6.3 0.9 copy.22
  7.7 0.6 copy-done.14
  8.3 1.2 copy-done.2
  9.6 0.9 copy-done.5
  10.5 0.8 copy-done.6
  11.3 7.5 %ssm_local.1 = (f32[256,2048]{1,0:T(8,128)S(1)}, f32[2,136,2048]{2,1,0:T(8,128)S(1)}) custom-call(bf16[256,2048]{1,0:T(8,128)(2,1)S(1)} %copy-done.2, bf16[256,512]{1,0:T(8,128)(2,1)S(1)} %copy-done.5, bf16[256,512]{1,0:T(8,128)(2,1)S(1)} %copy-done.4, f32[4,256,8]{2,1,0:T(8,128)S(1)} %bitcast.153, f32[4,256,8]{2,1,0:T(8,128)S(1)} %bitcast.151, ...), custom_call_target="tpu_custom_call" | custom-call | flops 400000000 | bytes 6291456 | tf_op jit(solution)/shard_map/ssm_local/pallas_call | solution.py:504
  18.8 1.3 %copy-done = f32[256,2048]{1,0:T(8,128)} copy-done((f32[256,2048]{1,0:T(8,128)}, f32[256,2048]{1,0:T(8,128)S(1)}, u32[]{:S(2)}) %copy-start) | copy-done | bytes 2097176
  20.2 1.1 constant_dynamic-slice_fusion
  21.5 0.7 pad_maximum_fusion.13
  22.1 0.8 constant_dynamic-slice_fusion.10
  23.0 0.4 collective-permute-start
  23.4 0.7 maximum_bitcast_fusion.6
  24.2 1.3 %dynamic-slice_bitcast_fusion.1 = (bf16[1,256,512]{2,1,0:T(8,128)(2,1)S(1)}, bf16[256,512]{1,0:T(8,128)(2,1)S(1)}) fusion(bf16[256,2048]{1,0:T(8,128)(2,1)} %param.12, s32[]{:T(128)S(6)} %dynamic_slice.67, s32[]{:T(128)S(6)} %dynamic_slice.63), kind=kLoop, calls=%fused_computation.95 | loop fusion | bytes 1048584 | tf_op jit(solution)/shard_map/stack | solution.py:488
  25.5 2.3 %collective-permute-done.4 = bf16[2,2,128,128]{3,2,1,0:T(8,128)(2,1)} collective-permute-done((bf16[2,2,128,128]{3,2,1,0:T(8,128)(2,1)}, bf16[2,2,128,128]{3,2,1,0:T(8,128)(2,1)}, u32[]{:S(2)}, u32[]{:S(2)}) %collective-permute-start.4) | collective-permute-done | bytes 131104 | tf_op jit(solution)/shard_map/ppermute | solution.py:461
  27.9 1.2 pad_maximum_fusion.2.refs_4_
  29.0 1.6 %collective-permute-start.7 = (bf16[2,4,2,128,128]{4,3,2,1,0:T(8,128)(2,1)S(1)}, bf16[2,4,2,128,128]{4,3,2,1,0:T(8,128)(2,1)S(1)}, u32[]{:S(2)}, u32[]{:S(2)}) collective-permute-start(bf16[2,4,2,128,128]{4,3,2,1,0:T(8,128)(2,1)S(1)} %pad_maximum_fusion.2.refs_4_), channel_id=1, source_target_pairs={{0,8},{2,10},{4,12},{6,14},{8,0},{10,2},{12,4},{14,6},{16,24},{18,... | collective-permute-start | bytes 1572872 | tf_op jit(solution)/shard_map/ppermute | solution.py:461
  30.7 2.6 %collective-permute-start.6 = (bf16[2,4,2,128,128]{4,3,2,1,0:T(8,128)(2,1)S(1)}, bf16[2,4,2,128,128]{4,3,2,1,0:T(8,128)(2,1)S(1)}, u32[]{:S(2)}, u32[]{:S(2)}) collective-permute-start(bf16[2,4,2,128,128]{4,3,2,1,0:T(8,128)(2,1)S(1)} %pad_maximum_fusion.2.refs_4_), channel_id=1, source_target_pairs={{0,16},{2,18},{4,20},{6,22},{8,24},{10,26},{12,28},{14,30},{16,0},... | collective-permute-start | bytes 1572872 | tf_op jit(solution)/shard_map/ppermute | solution.py:461
  33.6 0.5 collective-permute-start.1
  34.0 1.5 %dynamic-slice_select_fusion.1 = (f32[2,136,1024]{2,1,0:T(8,128)S(1)}, f32[2,136,1024]{2,1,0:T(8,128)S(1)}) fusion(f32[2,136,1024]{2,1,0:T(8,128)} %collective-permute-done.8, f32[2,136,2048]{2,1,0:T(8,128)S(1)} %get-tuple-element.13, s32[]{:T(128)S(6)} %select_n.419, pred[]{:T(512)S(6)} %eq.93), kind=kLoop, calls=%fused_computation.8 | loop fusion | flops 557056 | bytes 4456453 | tf_op jit(solution)/shard_map/jit(_where)/select_n | solution.py:529
  36.0 1.7 %collective-permute-start.9 = (bf16[2,144,512]{2,1,0:T(8,128)(2,1)S(1)}, bf16[2,144,512]{2,1,0:T(8,128)(2,1)S(1)}, u32[]{:S(2)}, u32[]{:S(2)}) collective-permute-start(bf16[2,144,512]{2,1,0:T(8,128)(2,1)S(1)} %fusion.13), channel_id=1, source_target_pairs={{0,4},{2,6},{4,0},{6,2},{8,12},{10,14},{12,8},{14,10},{16,20},{18,... | collective-permute-start | bytes 884744 | tf_op jit(solution)/shard_map/ppermute | solution.py:461
  37.7 10.8 %collective-permute-done.1 = bf16[2,256,512]{2,1,0:T(8,128)(2,1)S(1)} collective-permute-done((bf16[2,256,512]{2,1,0:T(8,128)(2,1)S(1)}, bf16[2,256,512]{2,1,0:T(8,128)(2,1)S(1)}, u32[]{:S(2)}, u32[]{:S(2)}) %collective-permute-start.1) | collective-permute-done | bytes 524320 | tf_op jit(solution)/shard_map/ppermute | solution.py:461
  48.5 11.5 %attn_local.1 = (f32[2,4,8,512]{3,2,1,0:T(8,128)S(1)}, f32[2,4,128,512]{3,2,1,0:T(8,128)S(1)}) custom-call(s32[2]{0:T(128)S(1)} %pad_add_fusion.place_ref, bf16[256,512]{1,0:T(8,128)(2,1)S(1)} %get-tuple-element.62.refs_0_, bf16[256,512]{1,0:T(8,128)(2,1)S(1)} %get-tuple-element.78.refs_1_, bf16[256,512]{1,0:T(8,128)(2,1)S(1)} %get-tuple-element.76.refs_2_, ...), custom_call_target="tpu_custom_call" | custom-call | flops 2000000000 | bytes 8388608 | tf_op jit(solution)/shard_map/attn_local/pallas_call | solution.py:616
  60.6 0.7 collective-permute-start.10
  61.4 6.5 %attn_remote.3 = (f32[2,4,8,512]{3,2,1,0:T(8,128)S(1)}, f32[2,4,128,512]{3,2,1,0:T(8,128)S(1)}) custom-call(s32[1]{0:T(128)} %bitcast.18.later_ref, bf16[256,512]{1,0:T(8,128)(2,1)S(1)} %get-tuple-element.62.refs_0_, bf16[256,512]{1,0:T(8,128)(2,1)S(1)} %get-tuple-element.78.refs_1_, ...), custom_call_target="tpu_custom_call", output_to_operand_aliasing={{0}: (6, {}), {1}: (7, {})} | custom-call | flops 2000000000 | bytes 8388608 | tf_op jit(solution)/shard_map/attn_remote/pallas_call | solution.py:616
  67.9 0.9 collective-permute-done.6.refs_4_
  68.9 6.5 %attn_remote.4 = (f32[2,4,8,512]{3,2,1,0:T(8,128)S(1)}, f32[2,4,128,512]{3,2,1,0:T(8,128)S(1)}) custom-call(s32[1]{0:T(128)} %bitcast.17.later_ref, bf16[256,512]{1,0:T(8,128)(2,1)S(1)} %get-tuple-element.62.refs_0_, bf16[256,512]{1,0:T(8,128)(2,1)S(1)} %get-tuple-element.78.refs_1_, ...), custom_call_target="tpu_custom_call", output_to_operand_aliasing={{0}: (6, {}), {1}: (7, {})} | custom-call | flops 2000000000 | bytes 8388608 | tf_op jit(solution)/shard_map/attn_remote/pallas_call | solution.py:616
  75.8 6.6 %attn_remote.5 = (f32[4,256,512]{2,1,0:T(8,128)S(1)}, f32[2,4,8,512]{3,2,1,0:T(8,128)S(1)}, f32[2,4,128,512]{3,2,1,0:T(8,128)S(1)}) custom-call(s32[1]{0:T(128)} %bitcast.later_ref, bf16[256,512]{1,0:T(8,128)(2,1)S(1)} %get-tuple-element.62.refs_0_, bf16[256,512]{1,0:T(8,128)(2,1)S(1)} %get-tuple-element.78.refs_1_, ...), custom_call_target="tpu_custom_call", output_to_operand_aliasing={{1}: (6, {}), {2}: (7, {})} | custom-call | flops 2000000000 | bytes 8388608 | tf_op jit(solution)/shard_map/attn_remote/pallas_call | solution.py:616
  82.6 0.6 collective-permute-start.11
  83.2 1.6 %collective-permute-start.13 = (bf16[256,512]{1,0:T(8,128)(2,1)S(1)}, bf16[256,512]{1,0:T(8,128)(2,1)S(1)}, u32[]{:S(2)}, u32[]{:S(2)}) collective-permute-start(bf16[256,512]{1,0:T(8,128)(2,1)S(1)} %get-tuple-element.59), channel_id=1, source_target_pairs={{0,6},{2,4},{4,2},{6,0},{8,14},{10,12},{12,10},{14,8},{16,22},{18,... | collective-permute-start | bytes 786440 | tf_op jit(solution)/shard_map/ppermute | solution.py:461
  85.2 5.0 %collective-permute-start.15 = (bf16[2,144,512]{2,1,0:T(8,128)(2,1)S(1)}, bf16[2,144,512]{2,1,0:T(8,128)(2,1)S(1)}, u32[]{:S(2)}, u32[]{:S(2)}) collective-permute-start(bf16[2,144,512]{2,1,0:T(8,128)(2,1)S(1)} %pad_maximum_fusion.8), channel_id=1, source_target_pairs={{0,16},{2,18},{4,20},{6,22},{8,24},{10,26},{12,28},{14,30},{16,0},... | collective-permute-start | bytes 884744 | tf_op jit(solution)/shard_map/ppermute | solution.py:461
  90.2 1.8 %collective-permute-done.11 = bf16[256,512]{1,0:T(8,128)(2,1)S(1)} collective-permute-done((bf16[256,512]{1,0:T(8,128)(2,1)S(1)}, bf16[256,512]{1,0:T(8,128)(2,1)S(1)}, u32[]{:S(2)}, u32[]{:S(2)}) %collective-permute-start.11) | collective-permute-done | bytes 262176 | tf_op jit(solution)/shard_map/ppermute | solution.py:461
  92.0 1.9 %collective-permute-done.13 = bf16[256,512]{1,0:T(8,128)(2,1)S(1)} collective-permute-done((bf16[256,512]{1,0:T(8,128)(2,1)S(1)}, bf16[256,512]{1,0:T(8,128)(2,1)S(1)}, u32[]{:S(2)}, u32[]{:S(2)}) %collective-permute-start.13) | collective-permute-done | bytes 262176 | tf_op jit(solution)/shard_map/ppermute | solution.py:461
  94.1 9.5 %collective-permute-done.15 = bf16[2,144,512]{2,1,0:T(8,128)(2,1)S(1)} collective-permute-done((bf16[2,144,512]{2,1,0:T(8,128)(2,1)S(1)}, bf16[2,144,512]{2,1,0:T(8,128)(2,1)S(1)}, u32[]{:S(2)}, u32[]{:S(2)}) %collective-permute-start.15) | collective-permute-done | bytes 294944 | tf_op jit(solution)/shard_map/ppermute | solution.py:461
  103.8 0.2 fusion.17
  104.1 0.6 collective-permute-start.16
  104.7 2.4 %fusion = f32[256,2048]{1,0:T(8,128)S(1)} fusion(bf16[2048,2048]{1,0:T(8,128)(2,1)S(1)} %bitcast.174, bf16[256,1024]{1,0:T(8,128)(2,1)S(1)} %get-tuple-element.57, bf16[256,1024]{1,0:T(8,128)(2,1)S(1)} %get-tuple-element.56), kind=kOutput, calls=%fused_computation | convolution fusion | flops 2149580800 | bytes 11534336 | tf_op jit(solution)/shard_map/dot_general | solution.py:643
  107.2 1.6 %collective-permute-start.14 = (bf16[256,1024]{1,0:T(8,128)(2,1)S(1)}, bf16[256,1024]{1,0:T(8,128)(2,1)S(1)}, u32[]{:S(2)}, u32[]{:S(2)}) collective-permute-start(bf16[256,1024]{1,0:T(8,128)(2,1)S(1)} %dynamic-slice_convert_fusion), channel_id=1, source_target_pairs={{0,1},{1,0},{2,3},{3,2},{4,5},{5,4},{6,7},{7,6},{8,9},{9,8},{10,11... | collective-permute-start | bytes 1572872 | tf_op jit(solution)/shard_map/ppermute | solution.py:646
  108.8 3.1 %collective-permute-done.16 = bf16[2,128,512]{2,1,0:T(8,128)(2,1)S(1)} collective-permute-done((bf16[2,128,512]{2,1,0:T(8,128)(2,1)S(1)}, bf16[2,128,512]{2,1,0:T(8,128)(2,1)S(1)}, u32[]{:S(2)}, u32[]{:S(2)}) %collective-permute-start.16) | collective-permute-done | bytes 262176 | tf_op jit(solution)/shard_map/ppermute | solution.py:461
  112.5 7.8 %collective-permute-done.14 = bf16[256,1024]{1,0:T(8,128)(2,1)S(1)} collective-permute-done((bf16[256,1024]{1,0:T(8,128)(2,1)S(1)}, bf16[256,1024]{1,0:T(8,128)(2,1)S(1)}, u32[]{:S(2)}, u32[]{:S(2)}) %collective-permute-start.14) | collective-permute-done | bytes 524320 | tf_op jit(solution)/shard_map/ppermute | solution.py:646
  120.3 2.4 %convert_add_fusion = f32[256,1024]{1,0:T(8,128)} fusion(bf16[256,1024]{1,0:T(8,128)(2,1)S(1)} %collective-permute-done.14, f32[256,2048]{1,0:T(8,128)} %copy-done.8, s32[]{:T(128)S(6)} %select_n.452), kind=kLoop, calls=%fused_computation.5 | loop fusion | flops 524288 | bytes 2621444 | tf_op jit(solution)/shard_map/add | solution.py:647
  122.7 1.3 broadcast_select_fusion.1
  124.1 0.3 copy-done.1
  124.4 0.3 copy-done.3
  124.7 5.9 %ssm_out.1 = f32[256,2048]{1,0:T(8,128)} custom-call(f32[256,2048]{1,0:T(8,128)S(1)} %copy-done.1, bf16[256,512]{1,0:T(8,128)(2,1)S(1)} %copy-done.4, f32[4,256,8]{2,1,0:T(8,128)S(1)} %bitcast.152, bf16[2,128,2048]{2,1,0:T(8,128)(2,1)S(1)} %pad_maximum_fusion.enter_ref, bf16[256,2048]{1,0:T(8,128)(2,1)S(1)} %copy-done.3, f32[4,1,512]{2,1,0:T(1,128)S(1)} %bitcast.156), custom_call_target="tpu_custom_call" | custom-call | flops 100000000 | bytes 6291456 | tf_op jit(solution)/shard_map/ssm_out/pallas_call | solution.py:584
  (114 shorter events, 3.9 us)
Async XLA Ops:
  0.6 6.6 %copy-start.15 = (f32[32,256]{1,0:T(8,128)S(1)}, f32[32,256]{1,0:T(8,128)}, u32[]{:S(2)}) copy-start(f32[32,256]{1,0:T(8,128)} %param.19) | copy-start | bytes 98308
  0.6 6.8 %copy-start.16 = (f32[32]{0:T(128)S(1)}, f32[32]{0:T(128)}, u32[]{:S(2)}) copy-start(f32[32]{0:T(128)} %param.21) | copy-start | bytes 388
  0.7 7.7 %copy-start.4 = (bf16[256,512]{1,0:T(8,128)(2,1)S(1)}, bf16[256,512]{1,0:T(8,128)(2,1)}, u32[]{:S(2)}) copy-start(bf16[256,512]{1,0:T(8,128)(2,1)} %read_ref.3) | copy-start | bytes 786436
  2.5 5.1 %collective-permute-start.2 = (bf16[2,2,128,128]{3,2,1,0:T(8,128)(2,1)S(1)}, bf16[2,2,128,128]{3,2,1,0:T(8,128)(2,1)S(1)}, u32[]{:S(2)}, u32[]{:S(2)}) collective-permute-start(bf16[2,2,128,128]{3,2,1,0:T(8,128)(2,1)S(1)} %pad_maximum_fusion.11), channel_id=1, source_target_pairs={{0,2},{2,0},{4,6},{6,4},{8,10},{10,8},{12,14},{14,12},{16,18},{18,... | collective-permute-start | bytes 393224 | tf_op jit(solution)/shard_map/ppermute | solution.py:461
  3.7 21.8 %collective-permute-start.3 = (bf16[2,2,128,128]{3,2,1,0:T(8,128)(2,1)}, bf16[2,2,128,128]{3,2,1,0:T(8,128)(2,1)}, u32[]{:S(2)}, u32[]{:S(2)}) collective-permute-start(bf16[2,2,128,128]{3,2,1,0:T(8,128)(2,1)} %pad_maximum_fusion.12), channel_id=1, source_target_pairs={{0,4},{2,6},{4,0},{6,2},{8,12},{10,14},{12,8},{14,10},{16,20},{18,... | collective-permute-start | bytes 393224 | tf_op jit(solution)/shard_map/ppermute | solution.py:461
  7.7 0.6 copy-start.14
  8.3 1.2 copy-start.2
  9.6 0.9 copy-start.5
  10.5 0.8 copy-start.6
  11.3 10.2 %copy-start.12 = (bf16[256,128]{1,0:T(8,128)(2,1)S(1)}, bf16[256,128]{1,0:T(8,128)(2,1)}, u32[]{:S(2)}) copy-start(bf16[256,128]{1,0:T(8,128)(2,1)} %get-tuple-element.85) | copy-start | bytes 196612
  11.3 10.2 %copy-start.13 = (bf16[256,128]{1,0:T(8,128)(2,1)S(1)}, bf16[256,128]{1,0:T(8,128)(2,1)}, u32[]{:S(2)}) copy-start(bf16[256,128]{1,0:T(8,128)(2,1)} %get-tuple-element.112) | copy-start | bytes 196612
  11.3 10.9 %copy-start.9 = (bf16[256,2048]{1,0:T(8,128)(2,1)S(1)}, bf16[256,2048]{1,0:T(8,128)(2,1)}, u32[]{:S(2)}) copy-start(bf16[256,2048]{1,0:T(8,128)(2,1)} %param.12) | copy-start | bytes 3145732
  18.8 1.4 %copy-start = (f32[256,2048]{1,0:T(8,128)}, f32[256,2048]{1,0:T(8,128)S(1)}, u32[]{:S(2)}) copy-start(f32[256,2048]{1,0:T(8,128)S(1)} %get-tuple-element.19.mixed_ref) | copy-start | bytes 6291460
  20.2 3.2 %copy-start.10 = (bf16[256,128]{1,0:T(8,128)(2,1)S(1)}, bf16[256,128]{1,0:T(8,128)(2,1)}, u32[]{:S(2)}) copy-start(bf16[256,128]{1,0:T(8,128)(2,1)} %get-tuple-element.83) | copy-start | bytes 196612
  20.2 3.2 %copy-start.11 = (bf16[256,128]{1,0:T(8,128)(2,1)S(1)}, bf16[256,128]{1,0:T(8,128)(2,1)}, u32[]{:S(2)}) copy-start(bf16[256,128]{1,0:T(8,128)(2,1)} %get-tuple-element.114) | copy-start | bytes 196612
  21.2 12.8 %collective-permute-start.8 = (f32[2,136,1024]{2,1,0:T(8,128)}, f32[2,136,1024]{2,1,0:T(8,128)}, u32[]{:S(2)}, u32[]{:S(2)}) collective-permute-start(f32[2,136,1024]{2,1,0:T(8,128)} %constant_dynamic-slice_fusion), channel_id=1, source_target_pairs={{0,2},{2,0},{4,6},{6,4},{8,10},{10,8},{12,14},{14,12},{16,18},{18,... | collective-permute-start | bytes 3342344 | tf_op jit(solution)/shard_map/ppermute | solution.py:461
  22.1 5.7 %collective-permute-start.4 = (bf16[2,2,128,128]{3,2,1,0:T(8,128)(2,1)}, bf16[2,2,128,128]{3,2,1,0:T(8,128)(2,1)}, u32[]{:S(2)}, u32[]{:S(2)}) collective-permute-start(bf16[2,2,128,128]{3,2,1,0:T(8,128)(2,1)} %pad_maximum_fusion.13), channel_id=1, source_target_pairs={{0,6},{2,4},{4,2},{6,0},{8,14},{10,12},{12,10},{14,8},{16,22},{18,... | collective-permute-start | bytes 393224 | tf_op jit(solution)/shard_map/ppermute | solution.py:461
  23.0 10.5 %collective-permute-start = (bf16[256,1024]{1,0:T(8,128)(2,1)}, bf16[256,1024]{1,0:T(8,128)(2,1)S(1)}, u32[]{:S(2)}, u32[]{:S(2)}) collective-permute-start(bf16[256,1024]{1,0:T(8,128)(2,1)} %constant_dynamic-slice_fusion.10), channel_id=1, source_target_pairs={{0,2},{2,0},{4,6},{6,4},{8,10},{10,8},{12,14},{14,12},{16,18},{18,... | collective-permute-start | bytes 1572872 | tf_op jit(solution)/shard_map/ppermute | solution.py:461
  29.0 32.3 %collective-permute-start.7 = (bf16[2,4,2,128,128]{4,3,2,1,0:T(8,128)(2,1)S(1)}, bf16[2,4,2,128,128]{4,3,2,1,0:T(8,128)(2,1)S(1)}, u32[]{:S(2)}, u32[]{:S(2)}) collective-permute-start(bf16[2,4,2,128,128]{4,3,2,1,0:T(8,128)(2,1)S(1)} %pad_maximum_fusion.2.refs_4_), channel_id=1, source_target_pairs={{0,8},{2,10},{4,12},{6,14},{8,0},{10,2},{12,4},{14,6},{16,24},{18,... | collective-permute-start | bytes 1572872 | tf_op jit(solution)/shard_map/ppermute | solution.py:461
  30.7 38.2 %collective-permute-start.6 = (bf16[2,4,2,128,128]{4,3,2,1,0:T(8,128)(2,1)S(1)}, bf16[2,4,2,128,128]{4,3,2,1,0:T(8,128)(2,1)S(1)}, u32[]{:S(2)}, u32[]{:S(2)}) collective-permute-start(bf16[2,4,2,128,128]{4,3,2,1,0:T(8,128)(2,1)S(1)} %pad_maximum_fusion.2.refs_4_), channel_id=1, source_target_pairs={{0,16},{2,18},{4,20},{6,22},{8,24},{10,26},{12,28},{14,30},{16,0},... | collective-permute-start | bytes 1572872 | tf_op jit(solution)/shard_map/ppermute | solution.py:461
  33.2 42.5 %collective-permute-start.5 = (bf16[2,4,2,128,128]{4,3,2,1,0:T(8,128)(2,1)S(1)}, bf16[2,4,2,128,128]{4,3,2,1,0:T(8,128)(2,1)S(1)}, u32[]{:S(2)}, u32[]{:S(2)}) collective-permute-start(bf16[2,4,2,128,128]{4,3,2,1,0:T(8,128)(2,1)S(1)} %pad_maximum_fusion.2.refs_4_), channel_id=1, source_target_pairs={{0,24},{2,26},{4,28},{6,30},{8,16},{10,18},{12,20},{14,22},{16,8},... | collective-permute-start | bytes 1572872 | tf_op jit(solution)/shard_map/ppermute | solution.py:461
  33.6 14.9 %collective-permute-start.1 = (bf16[2,256,512]{2,1,0:T(8,128)(2,1)S(1)}, bf16[2,256,512]{2,1,0:T(8,128)(2,1)S(1)}, u32[]{:S(2)}, u32[]{:S(2)}) collective-permute-start(bf16[2,256,512]{2,1,0:T(8,128)(2,1)S(1)} %pad_maximum_fusion.1), channel_id=1, source_target_pairs={{0,4},{2,6},{4,0},{6,2},{8,12},{10,14},{12,8},{14,10},{16,20},{18,... | collective-permute-start | bytes 1572872 | tf_op jit(solution)/shard_map/ppermute | solution.py:461
  36.0 24.1 %collective-permute-start.9 = (bf16[2,144,512]{2,1,0:T(8,128)(2,1)S(1)}, bf16[2,144,512]{2,1,0:T(8,128)(2,1)S(1)}, u32[]{:S(2)}, u32[]{:S(2)}) collective-permute-start(bf16[2,144,512]{2,1,0:T(8,128)(2,1)S(1)} %fusion.13), channel_id=1, source_target_pairs={{0,4},{2,6},{4,0},{6,2},{8,12},{10,14},{12,8},{14,10},{16,20},{18,... | collective-permute-start | bytes 884744 | tf_op jit(solution)/shard_map/ppermute | solution.py:461
  60.6 14.8 %collective-permute-start.10 = (bf16[2,144,512]{2,1,0:T(8,128)(2,1)S(1)}, bf16[2,144,512]{2,1,0:T(8,128)(2,1)S(1)}, u32[]{:S(2)}, u32[]{:S(2)}) collective-permute-start(bf16[2,144,512]{2,1,0:T(8,128)(2,1)S(1)} %pad_maximum_fusion.7), channel_id=1, source_target_pairs={{0,8},{2,10},{4,12},{6,14},{8,0},{10,2},{12,4},{14,6},{16,24},{18,... | collective-permute-start | bytes 884744 | tf_op jit(solution)/shard_map/ppermute | solution.py:461
  75.8 28.9 %slice-start = ((s8[8388608]{0:T(1024)(128)(4,1)}), s8[4194304]{0:T(1024)(128)(4,1)S(1)}, s32[]{:S(2)}) async-start(s8[8388608]{0:T(1024)(128)(4,1)} %bitcast.173), calls=%async_computation | async-start | bytes 8388608
  82.6 22.1 %slice-start.1 = ((s8[8388608]{0:T(1024)(128)(4,1)}), s8[4194304]{0:T(1024)(128)(4,1)S(1)}, s32[]{:S(2)}) async-start(s8[8388608]{0:T(1024)(128)(4,1)} %bitcast.173), calls=%async_computation.1 | async-start | bytes 8388608
  82.6 9.3 %collective-permute-start.11 = (bf16[256,512]{1,0:T(8,128)(2,1)S(1)}, bf16[256,512]{1,0:T(8,128)(2,1)S(1)}, u32[]{:S(2)}, u32[]{:S(2)}) collective-permute-start(bf16[256,512]{1,0:T(8,128)(2,1)S(1)} %get-tuple-element.58), channel_id=1, source_target_pairs={{0,4},{2,6},{4,0},{6,2},{8,12},{10,14},{12,8},{14,10},{16,20},{18,... | collective-permute-start | bytes 786440 | tf_op jit(solution)/shard_map/ppermute | solution.py:461
  83.2 8.8 %collective-permute-start.12 = (bf16[256,512]{1,0:T(8,128)(2,1)S(1)}, bf16[256,512]{1,0:T(8,128)(2,1)S(1)}, u32[]{:S(2)}, u32[]{:S(2)}) collective-permute-start(bf16[256,512]{1,0:T(8,128)(2,1)S(1)} %get-tuple-element.60), channel_id=1, source_target_pairs={{0,2},{2,0},{4,6},{6,4},{8,10},{10,8},{12,14},{14,12},{16,18},{18,... | collective-permute-start | bytes 786440 | tf_op jit(solution)/shard_map/ppermute | solution.py:461
  83.2 10.7 %collective-permute-start.13 = (bf16[256,512]{1,0:T(8,128)(2,1)S(1)}, bf16[256,512]{1,0:T(8,128)(2,1)S(1)}, u32[]{:S(2)}, u32[]{:S(2)}) collective-permute-start(bf16[256,512]{1,0:T(8,128)(2,1)S(1)} %get-tuple-element.59), channel_id=1, source_target_pairs={{0,6},{2,4},{4,2},{6,0},{8,14},{10,12},{12,10},{14,8},{16,22},{18,... | collective-permute-start | bytes 786440 | tf_op jit(solution)/shard_map/ppermute | solution.py:461
  85.2 18.5 %collective-permute-start.15 = (bf16[2,144,512]{2,1,0:T(8,128)(2,1)S(1)}, bf16[2,144,512]{2,1,0:T(8,128)(2,1)S(1)}, u32[]{:S(2)}, u32[]{:S(2)}) collective-permute-start(bf16[2,144,512]{2,1,0:T(8,128)(2,1)S(1)} %pad_maximum_fusion.8), channel_id=1, source_target_pairs={{0,16},{2,18},{4,20},{6,22},{8,24},{10,26},{12,28},{14,30},{16,0},... | collective-permute-start | bytes 884744 | tf_op jit(solution)/shard_map/ppermute | solution.py:461
  104.1 7.7 %collective-permute-start.16 = (bf16[2,128,512]{2,1,0:T(8,128)(2,1)S(1)}, bf16[2,128,512]{2,1,0:T(8,128)(2,1)S(1)}, u32[]{:S(2)}, u32[]{:S(2)}) collective-permute-start(bf16[2,128,512]{2,1,0:T(8,128)(2,1)S(1)} %broadcast_select_fusion.10), channel_id=1, source_target_pairs={{0,4},{2,6},{4,0},{6,2},{8,12},{10,14},{12,8},{14,10},{16,20},{18,... | collective-permute-start | bytes 786440 | tf_op jit(solution)/shard_map/ppermute | solution.py:461
  107.1 5.2 %copy-start.8 = (f32[256,2048]{1,0:T(8,128)}, f32[256,2048]{1,0:T(8,128)S(1)}, u32[]{:S(2)}) copy-start(f32[256,2048]{1,0:T(8,128)S(1)} %fusion) | copy-start | bytes 6291460
  107.2 13.1 %collective-permute-start.14 = (bf16[256,1024]{1,0:T(8,128)(2,1)S(1)}, bf16[256,1024]{1,0:T(8,128)(2,1)S(1)}, u32[]{:S(2)}, u32[]{:S(2)}) collective-permute-start(bf16[256,1024]{1,0:T(8,128)(2,1)S(1)} %dynamic-slice_convert_fusion), channel_id=1, source_target_pairs={{0,1},{1,0},{2,3},{3,2},{4,5},{5,4},{6,7},{7,6},{8,9},{9,8},{10,11... | collective-permute-start | bytes 1572872 | tf_op jit(solution)/shard_map/ppermute | solution.py:646
  112.4 10.2 %collective-permute-start.17 = (bf16[2,128,1024]{2,1,0:T(8,128)(2,1)S(1)}, bf16[2,128,1024]{2,1,0:T(8,128)(2,1)}, u32[]{:S(2)}, u32[]{:S(2)}) collective-permute-start(bf16[2,128,1024]{2,1,0:T(8,128)(2,1)S(1)} %broadcast_select_fusion.2), channel_id=1, source_target_pairs={{0,2},{2,0},{4,6},{6,4},{8,10},{10,8},{12,14},{14,12},{16,18},{18,... | collective-permute-start | bytes 1572872 | tf_op jit(solution)/shard_map/ppermute | solution.py:461
  122.7 1.7 %copy-start.1 = (f32[256,2048]{1,0:T(8,128)S(1)}, f32[256,2048]{1,0:T(8,128)}, u32[]{:S(2)}) copy-start(f32[256,2048]{1,0:T(8,128)} %copy-done) | copy-start | bytes 6291460
  122.7 2.0 %copy-start.3 = (bf16[256,2048]{1,0:T(8,128)(2,1)S(1)}, bf16[256,2048]{1,0:T(8,128)(2,1)}, u32[]{:S(2)}) copy-start(bf16[256,2048]{1,0:T(8,128)(2,1)} %gate_ref.1) | copy-start | bytes 3145732
  122.7 2.0 %copy-start.7 = (f32[2048]{0:T(1024)S(1)}, f32[2048]{0:T(1024)}, u32[]{:S(2)}) copy-start(f32[2048]{0:T(1024)} %param.22) | copy-start | bytes 24580

commit v3 on v2

--- a/solution.py
+++ b/solution.py
@@ -634,17 +634,17 @@
             functools.partial(attn_remote_kernel, last), "attn_remote", later, kv_from[by], states, waits, last
         )
         states = [stat, acc]
-    heads_plane = result[0].astype(BF16)
+    heads_plane = (result[0] + z_came[-1][0, -1, :1].astype(F32)).astype(BF16)
 
     pieces = [heads_plane[0]] + [send(heads_plane[k], near_pairs[k]) for k in (1, 2, 3)]
     attn_heads = in_order(
         in_order(pieces[0], pieces[2], y, axis=1), in_order(pieces[1], pieces[3], y, axis=1), core, axis=1
     )
-    head_terms = jnp.dot(attn_heads, out_weight, preferred_element_type=F32)
     out_cols = out_weight.shape[1] // 2
-    away = part(head_terms, 1 - tp_index, out_cols, 1).astype(BF16)
-    came = lax.ppermute(away, "tp", [(0, 1), (1, 0)])
-    attn_mixed = part(head_terms, tp_index, out_cols, 1) + came.astype(F32)
+    away = jnp.dot(attn_heads, part(out_weight, 1 - tp_index, out_cols, 1), preferred_element_type=F32)
+    came = lax.ppermute(away.astype(BF16), "tp", [(0, 1), (1, 0)])
+    mine = jnp.dot(attn_heads, part(out_weight, tp_index, out_cols, 1), preferred_element_type=F32)
+    attn_mixed = lax.optimization_barrier(mine) + came.astype(F32)
     return attn_mixed, ssm_output
 
 

time: 131 us -> 128 us (0.977)
  waiting for transfers between devices: 38.1 us -> 33.6 us
  starting transfers between devices: 20.4 us -> 17.9 us
  local copies, waits for them, and re-layouts: 12.3 us -> 14.7 us
    ppermute x1, waiting for transfers between devices: 7.75 us -> 3.85 us  [split_body(): came = lax.ppermute(away.astype(BF16), 'tp', [(0, 1), (1, 0)])]
    ppermute x17, starting transfers between devices: 18.8 us -> 16.4 us  [send(): return lax.ppermute(x, 'ctx', pairs)]
    unnamed x38 -> x40, local copies, waits for them, and re-layouts: 5.57 us -> 7.44 us
    another operation x3, other arithmetic: 0.55 us -> 1.9 us
  transfers between devices with their start and end apart: 18 -> 18, of which waited for: 8 -> 8; matrix products, arithmetic and copies ran while one was open for 13% -> 14% of each run, Pallas kernels for 25% -> 35%
where the time goes in v3:
time: 128 us
  Pallas kernels  44.7 us (35%)
  waiting for transfers between devices  33.6 us (26%)
  starting transfers between devices  17.9 us (14%)
  local copies, waits for them, and re-layouts  14.7 us (11%)
  other arithmetic  12.1 us (9%)
  matrix products  2.54 us (2%)
  between operations  2.02 us (2%)
    pallas_call x4, Pallas kernels, attend(): pl.pallas_call(kernel, in_specs=[smem] + [VMEM_SPEC] * (5 + len(states))...  31.2 us
    ppermute x17, waiting for transfers between devices, send(): return lax.ppermute(x, 'ctx', pairs)  29.8 us
    ppermute x17, starting transfers between devices, send(): return lax.ppermute(x, 'ctx', pairs)  16.4 us
    pallas_call x1, Pallas kernels, split_body(): pl.pallas_call(ssm_local_kernel, grid=(2, groups), in_specs=[wide, narrow...  7.53 us
    unnamed x40, local copies, waits for them, and re-layouts  7.44 us
    pallas_call x1, Pallas kernels, split_body(): pl.pallas_call(ssm_out_kernel, grid=(2, groups), in_specs=[wide, narrow,...  5.92 us
    ppermute x1, waiting for transfers between devices, split_body(): came = lax.ppermute(away.astype(BF16), 'tp', [(0, 1), (1, 0)])  3.85 us
    dynamic_slice x3, local copies, waits for them, and re-layouts, part(): return lax.dynamic_slice_in_dim(x, which * width, width, axis)  3.74 us
  transfers between devices with their start and end apart: 18, of which 8 were waited for; matrix products, arithmetic and copies ran while one was open for 14% of the time, Pallas kernels for 35%

profile of v3, /device:TPU:0, one launch (start us, length us, event | category | flops | bytes accessed | tf_op | source)
XLA Modules:
  0.0 127.5 jit_solution(16452277585316751120)
XLA Ops:
  0.7 1.8 %constant_dynamic-slice_fusion.7 = (bf16[256,128]{1,0:T(8,128)(2,1)}, bf16[256,128]{1,0:T(8,128)(2,1)S(1)}, bf16[256,128]{1,0:T(8,128)(2,1)}, bf16[256,128]{1,0:...) fusion(bf16[256,512]{1,0:T(8,128)(2,1)} %param.14, ...), kind=kLoop, calls=%fused_computation.141 | loop fusion | bytes 1048592 | tf_op jit(solution)/shard_map/dynamic_slice | solution.py:464
  2.5 0.5 collective-permute-start.2
  3.0 0.7 pad_maximum_fusion.15
  3.7 2.5 %collective-permute-start.3 = (bf16[2,2,128,128]{3,2,1,0:T(8,128)(2,1)}, bf16[2,2,128,128]{3,2,1,0:T(8,128)(2,1)}, u32[]{:S(2)}, u32[]{:S(2)}) collective-permute-start(bf16[2,2,128,128]{3,2,1,0:T(8,128)(2,1)} %pad_maximum_fusion.15), channel_id=1, source_target_pairs={{0,4},{2,6},{4,0},{6,2},{8,12},{10,14},{12,8},{14,10},{16,20},{18,... | collective-permute-start | bytes 393224 | tf_op jit(solution)/shard_map/ppermute | solution.py:461
  6.2 0.9 copy.22
  7.7 0.6 copy-done.15
  8.3 1.2 copy-done.2
  9.5 0.9 copy-done.5
  10.5 0.8 copy-done.6
  11.2 7.5 %ssm_local.1 = (f32[256,2048]{1,0:T(8,128)S(1)}, f32[2,136,2048]{2,1,0:T(8,128)S(1)}) custom-call(bf16[256,2048]{1,0:T(8,128)(2,1)S(1)} %copy-done.2, bf16[256,512]{1,0:T(8,128)(2,1)S(1)} %copy-done.5, bf16[256,512]{1,0:T(8,128)(2,1)S(1)} %copy-done.4, f32[4,256,8]{2,1,0:T(8,128)S(1)} %bitcast.154, f32[4,256,8]{2,1,0:T(8,128)S(1)} %bitcast.152, ...), custom_call_target="tpu_custom_call" | custom-call | flops 400000000 | bytes 6291456 | tf_op jit(solution)/shard_map/ssm_local/pallas_call | solution.py:504
  18.8 1.3 %copy-done = f32[256,2048]{1,0:T(8,128)} copy-done((f32[256,2048]{1,0:T(8,128)}, f32[256,2048]{1,0:T(8,128)S(1)}, u32[]{:S(2)}) %copy-start) | copy-done | bytes 2097176
  20.1 1.1 constant_dynamic-slice_fusion
  21.4 0.7 pad_maximum_fusion.16
  22.1 0.8 constant_dynamic-slice_fusion.10
  23.4 0.7 maximum_bitcast_fusion.6
  24.1 1.3 %dynamic-slice_bitcast_fusion.1 = (bf16[1,256,512]{2,1,0:T(8,128)(2,1)S(1)}, bf16[256,512]{1,0:T(8,128)(2,1)S(1)}) fusion(bf16[256,2048]{1,0:T(8,128)(2,1)} %param.12, s32[]{:T(128)S(6)} %dynamic_slice.67, s32[]{:T(128)S(6)} %dynamic_slice.63), kind=kLoop, calls=%fused_computation.97 | loop fusion | bytes 1048584 | tf_op jit(solution)/shard_map/stack | solution.py:488
  25.5 2.3 %collective-permute-done.4 = bf16[2,2,128,128]{3,2,1,0:T(8,128)(2,1)} collective-permute-done((bf16[2,2,128,128]{3,2,1,0:T(8,128)(2,1)}, bf16[2,2,128,128]{3,2,1,0:T(8,128)(2,1)}, u32[]{:S(2)}, u32[]{:S(2)}) %collective-permute-start.4) | collective-permute-done | bytes 131104 | tf_op jit(solution)/shard_map/ppermute | solution.py:461
  27.8 1.2 pad_maximum_fusion.5.refs_4_
  29.0 1.6 %collective-permute-start.7 = (bf16[2,4,2,128,128]{4,3,2,1,0:T(8,128)(2,1)S(1)}, bf16[2,4,2,128,128]{4,3,2,1,0:T(8,128)(2,1)S(1)}, u32[]{:S(2)}, u32[]{:S(2)}) collective-permute-start(bf16[2,4,2,128,128]{4,3,2,1,0:T(8,128)(2,1)S(1)} %pad_maximum_fusion.5.refs_4_), channel_id=1, source_target_pairs={{0,8},{2,10},{4,12},{6,14},{8,0},{10,2},{12,4},{14,6},{16,24},{18,... | collective-permute-start | bytes 1572872 | tf_op jit(solution)/shard_map/ppermute | solution.py:461
  30.6 2.6 %collective-permute-start.6 = (bf16[2,4,2,128,128]{4,3,2,1,0:T(8,128)(2,1)S(1)}, bf16[2,4,2,128,128]{4,3,2,1,0:T(8,128)(2,1)S(1)}, u32[]{:S(2)}, u32[]{:S(2)}) collective-permute-start(bf16[2,4,2,128,128]{4,3,2,1,0:T(8,128)(2,1)S(1)} %pad_maximum_fusion.5.refs_4_), channel_id=1, source_target_pairs={{0,16},{2,18},{4,20},{6,22},{8,24},{10,26},{12,28},{14,30},{16,0},... | collective-permute-start | bytes 1572872 | tf_op jit(solution)/shard_map/ppermute | solution.py:461
  34.0 1.5 %dynamic-slice_select_fusion.1 = (f32[2,136,1024]{2,1,0:T(8,128)S(1)}, f32[2,136,1024]{2,1,0:T(8,128)S(1)}) fusion(f32[2,136,1024]{2,1,0:T(8,128)} %collective-permute-done.8, f32[2,136,2048]{2,1,0:T(8,128)S(1)} %get-tuple-element.13, s32[]{:T(128)S(6)} %select_n.419, pred[]{:T(512)S(6)} %eq.93), kind=kLoop, calls=%fused_computation.10 | loop fusion | flops 557056 | bytes 4456453 | tf_op jit(solution)/shard_map/jit(_where)/select_n | solution.py:529
  36.0 0.6 copy-done.8
  36.9 1.6 %collective-permute-start.9 = (bf16[2,144,512]{2,1,0:T(8,128)(2,1)S(1)}, bf16[2,144,512]{2,1,0:T(8,128)(2,1)S(1)}, u32[]{:S(2)}, u32[]{:S(2)}) collective-permute-start(bf16[2,144,512]{2,1,0:T(8,128)(2,1)S(1)} %fusion.16), channel_id=1, source_target_pairs={{0,4},{2,6},{4,0},{6,2},{8,12},{10,14},{12,8},{14,10},{16,20},{18,... | collective-permute-start | bytes 884744 | tf_op jit(solution)/shard_map/ppermute | solution.py:461
  38.5 9.9 %collective-permute-done.1 = bf16[2,256,512]{2,1,0:T(8,128)(2,1)S(1)} collective-permute-done((bf16[2,256,512]{2,1,0:T(8,128)(2,1)S(1)}, bf16[2,256,512]{2,1,0:T(8,128)(2,1)S(1)}, u32[]{:S(2)}, u32[]{:S(2)}) %collective-permute-start.1) | collective-permute-done | bytes 524320 | tf_op jit(solution)/shard_map/ppermute | solution.py:461
  48.5 11.5 %attn_local.1 = (f32[2,4,8,512]{3,2,1,0:T(8,128)S(1)}, f32[2,4,128,512]{3,2,1,0:T(8,128)S(1)}) custom-call(s32[2]{0:T(128)S(1)} %pad_add_fusion.place_ref, bf16[256,512]{1,0:T(8,128)(2,1)S(1)} %get-tuple-element.62.refs_0_, bf16[256,512]{1,0:T(8,128)(2,1)S(1)} %get-tuple-element.78.refs_1_, bf16[256,512]{1,0:T(8,128)(2,1)S(1)} %get-tuple-element.76.refs_2_, ...), custom_call_target="tpu_custom_call" | custom-call | flops 2000000000 | bytes 8388608 | tf_op jit(solution)/shard_map/attn_local/pallas_call | solution.py:616
  60.6 0.7 collective-permute-start.10
  61.3 6.5 %attn_remote.3 = (f32[2,4,8,512]{3,2,1,0:T(8,128)S(1)}, f32[2,4,128,512]{3,2,1,0:T(8,128)S(1)}) custom-call(s32[1]{0:T(128)} %bitcast.18.later_ref, bf16[256,512]{1,0:T(8,128)(2,1)S(1)} %get-tuple-element.62.refs_0_, bf16[256,512]{1,0:T(8,128)(2,1)S(1)} %get-tuple-element.78.refs_1_, ...), custom_call_target="tpu_custom_call", output_to_operand_aliasing={{0}: (6, {}), {1}: (7, {})} | custom-call | flops 2000000000 | bytes 8388608 | tf_op jit(solution)/shard_map/attn_remote/pallas_call | solution.py:616
  67.9 1.0 collective-permute-done.6.refs_4_
  68.8 6.5 %attn_remote.4 = (f32[2,4,8,512]{3,2,1,0:T(8,128)S(1)}, f32[2,4,128,512]{3,2,1,0:T(8,128)S(1)}) custom-call(s32[1]{0:T(128)} %bitcast.17.later_ref, bf16[256,512]{1,0:T(8,128)(2,1)S(1)} %get-tuple-element.62.refs_0_, bf16[256,512]{1,0:T(8,128)(2,1)S(1)} %get-tuple-element.78.refs_1_, ...), custom_call_target="tpu_custom_call", output_to_operand_aliasing={{0}: (6, {}), {1}: (7, {})} | custom-call | flops 2000000000 | bytes 8388608 | tf_op jit(solution)/shard_map/attn_remote/pallas_call | solution.py:616
  76.1 2.6 %collective-permute-start.11 = (bf16[2,144,512]{2,1,0:T(8,128)(2,1)S(1)}, bf16[2,144,512]{2,1,0:T(8,128)(2,1)S(1)}, u32[]{:S(2)}, u32[]{:S(2)}) collective-permute-start(bf16[2,144,512]{2,1,0:T(8,128)(2,1)S(1)} %pad_maximum_fusion.11), channel_id=1, source_target_pairs={{0,16},{2,18},{4,20},{6,22},{8,24},{10,26},{12,28},{14,30},{16,0},... | collective-permute-start | bytes 884744 | tf_op jit(solution)/shard_map/ppermute | solution.py:461
  78.7 6.6 %attn_remote.5 = (f32[4,256,512]{2,1,0:T(8,128)S(1)}, f32[2,4,8,512]{3,2,1,0:T(8,128)S(1)}, f32[2,4,128,512]{3,2,1,0:T(8,128)S(1)}) custom-call(s32[1]{0:T(128)} %bitcast.later_ref, bf16[256,512]{1,0:T(8,128)(2,1)S(1)} %get-tuple-element.62.refs_0_, bf16[256,512]{1,0:T(8,128)(2,1)S(1)} %get-tuple-element.78.refs_1_, ...), custom_call_target="tpu_custom_call", output_to_operand_aliasing={{1}: (6, {}), {2}: (7, {})} | custom-call | flops 2000000000 | bytes 8388608 | tf_op jit(solution)/shard_map/attn_remote/pallas_call | solution.py:616
  85.3 6.4 %collective-permute-done.11 = bf16[2,144,512]{2,1,0:T(8,128)(2,1)S(1)} collective-permute-done((bf16[2,144,512]{2,1,0:T(8,128)(2,1)S(1)}, bf16[2,144,512]{2,1,0:T(8,128)(2,1)S(1)}, u32[]{:S(2)}, u32[]{:S(2)}) %collective-permute-start.11) | collective-permute-done | bytes 294944 | tf_op jit(solution)/shard_map/ppermute | solution.py:461
  92.1 0.8 broadcast_select_fusion.10
  93.4 0.6 slice.255
  95.0 1.6 %collective-permute-start.12 = (bf16[256,512]{1,0:T(8,128)(2,1)S(1)}, bf16[256,512]{1,0:T(8,128)(2,1)S(1)}, u32[]{:S(2)}, u32[]{:S(2)}) collective-permute-start(bf16[256,512]{1,0:T(8,128)(2,1)S(1)} %get-tuple-element.58), channel_id=1, source_target_pairs={{0,4},{2,6},{4,0},{6,2},{8,12},{10,14},{12,8},{14,10},{16,20},{18,... | collective-permute-start | bytes 786440 | tf_op jit(solution)/shard_map/ppermute | solution.py:461
  96.5 0.6 collective-permute-start.14
  97.2 5.3 %collective-permute-done.16 = bf16[2,128,512]{2,1,0:T(8,128)(2,1)} collective-permute-done((bf16[2,128,512]{2,1,0:T(8,128)(2,1)}, bf16[2,128,512]{2,1,0:T(8,128)(2,1)}, u32[]{:S(2)}, u32[]{:S(2)}) %collective-permute-start.16) | collective-permute-done | bytes 262176 | tf_op jit(solution)/shard_map/ppermute | solution.py:461
  102.4 1.0 broadcast_select_fusion.9
  103.6 1.6 %add_convert_fusion.2 = (bf16[1,128,1024]{2,1,0:T(8,128)(2,1)S(1)}, bf16[1,128,1024]{2,1,0:T(8,128)(2,1)S(1)}) fusion(f32[2,128,1024]{2,1,0:T(8,128)S(1)} %maximum_convert_fusion, f32[2,136,1024]{2,1,0:T(8,128)} %copy-done.8, f32[1024]{0:T(1024)S(1)} %bitcast.168, f32[2,136,1024]{2,1,0:T(8,128)} %copy-done.9, f32[1024]{0:T(1024)S(1)} %bitcast.169), kind=kLoop, calls=%fused_computation.31 | loop fusion | flops 786432 | bytes 2629632 | tf_op jit(solution)/shard_map/convert.13
  105.4 2.5 %collective-permute-done.12 = bf16[256,512]{1,0:T(8,128)(2,1)S(1)} collective-permute-done((bf16[256,512]{1,0:T(8,128)(2,1)S(1)}, bf16[256,512]{1,0:T(8,128)(2,1)S(1)}, u32[]{:S(2)}, u32[]{:S(2)}) %collective-permute-start.12) | collective-permute-done | bytes 262176 | tf_op jit(solution)/shard_map/ppermute | solution.py:461
  108.0 2.3 %collective-permute-done.14 = bf16[256,512]{1,0:T(8,128)(2,1)S(1)} collective-permute-done((bf16[256,512]{1,0:T(8,128)(2,1)S(1)}, bf16[256,512]{1,0:T(8,128)(2,1)S(1)}, u32[]{:S(2)}, u32[]{:S(2)}) %collective-permute-start.14) | collective-permute-done | bytes 262176 | tf_op jit(solution)/shard_map/ppermute | solution.py:461
  110.6 1.3 %fusion.4 = bf16[256,1024]{1,0:T(8,128)(2,1)S(1)} fusion(bf16[2048,2048]{1,0:T(8,128)(2,1)S(1)} %bitcast.175, s32[]{:T(128)S(6)} %select_n.470, bf16[256,1024]{1,0:T(8,128)(2,1)S(1)} %get-tuple-element.57, bf16[256,1024]{1,0:T(8,128)(2,1)S(1)} %get-tuple-element.56), kind=kOutput, calls=%fused_computation.5 | convolution fusion | flops 1076101120 | bytes 5767172 | tf_op jit(solution)/shard_map/dot_general | solution.py:644
  111.9 1.6 %collective-permute-start.15 = (bf16[256,1024]{1,0:T(8,128)(2,1)S(1)}, bf16[256,1024]{1,0:T(8,128)(2,1)S(1)}, u32[]{:S(2)}, u32[]{:S(2)}) collective-permute-start(bf16[256,1024]{1,0:T(8,128)(2,1)S(1)} %fusion.4), channel_id=1, source_target_pairs={{0,1},{1,0},{2,3},{3,2},{4,5},{5,4},{6,7},{7,6},{8,9},{9,8},{10,11... | collective-permute-start | bytes 1572872 | tf_op jit(solution)/shard_map/ppermute | solution.py:645
  113.5 1.3 fusion.2
  115.0 1.3 %copy-done.1 = f32[256,2048]{1,0:T(8,128)S(1)} copy-done((f32[256,2048]{1,0:T(8,128)S(1)}, f32[256,2048]{1,0:T(8,128)}, u32[]{:S(2)}) %copy-start.1) | copy-done | bytes 2097176
  116.6 5.9 %ssm_out.1 = f32[256,2048]{1,0:T(8,128)} custom-call(f32[256,2048]{1,0:T(8,128)S(1)} %copy-done.1, bf16[256,512]{1,0:T(8,128)(2,1)S(1)} %copy-done.4, f32[4,256,8]{2,1,0:T(8,128)S(1)} %bitcast.153, bf16[2,128,2048]{2,1,0:T(8,128)(2,1)S(1)} %pad_maximum_fusion.1.enter_ref, bf16[256,2048]{1,0:T(8,128)(2,1)S(1)} %copy-done.3, f32[4,1,512]{2,1,0:T(1,128)S(1)} %bitcast.157), custom_call_target="tpu_custom_call" | custom-call | flops 100000000 | bytes 6291456 | tf_op jit(solution)/shard_map/ssm_out/pallas_call | solution.py:584
  122.5 3.8 %collective-permute-done.15 = bf16[256,1024]{1,0:T(8,128)(2,1)S(1)} collective-permute-done((bf16[256,1024]{1,0:T(8,128)(2,1)S(1)}, bf16[256,1024]{1,0:T(8,128)(2,1)S(1)}, u32[]{:S(2)}, u32[]{:S(2)}) %collective-permute-start.15) | collective-permute-done | bytes 524320 | tf_op jit(solution)/shard_map/ppermute | solution.py:645
  126.4 1.2 convert_add_fusion
  (117 shorter events, 6.2 us)
Async XLA Ops:
  0.6 6.6 %copy-start.16 = (f32[32,256]{1,0:T(8,128)S(1)}, f32[32,256]{1,0:T(8,128)}, u32[]{:S(2)}) copy-start(f32[32,256]{1,0:T(8,128)} %param.19) | copy-start | bytes 98308
  0.6 6.8 %copy-start.17 = (f32[32]{0:T(128)S(1)}, f32[32]{0:T(128)}, u32[]{:S(2)}) copy-start(f32[32]{0:T(128)} %param.21) | copy-start | bytes 388
  0.7 7.6 %copy-start.4 = (bf16[256,512]{1,0:T(8,128)(2,1)S(1)}, bf16[256,512]{1,0:T(8,128)(2,1)}, u32[]{:S(2)}) copy-start(bf16[256,512]{1,0:T(8,128)(2,1)} %read_ref.3) | copy-start | bytes 786436
  2.5 5.1 %collective-permute-start.2 = (bf16[2,2,128,128]{3,2,1,0:T(8,128)(2,1)S(1)}, bf16[2,2,128,128]{3,2,1,0:T(8,128)(2,1)S(1)}, u32[]{:S(2)}, u32[]{:S(2)}) collective-permute-start(bf16[2,2,128,128]{3,2,1,0:T(8,128)(2,1)S(1)} %pad_maximum_fusion.14), channel_id=1, source_target_pairs={{0,2},{2,0},{4,6},{6,4},{8,10},{10,8},{12,14},{14,12},{16,18},{18,... | collective-permute-start | bytes 393224 | tf_op jit(solution)/shard_map/ppermute | solution.py:461
  3.7 21.8 %collective-permute-start.3 = (bf16[2,2,128,128]{3,2,1,0:T(8,128)(2,1)}, bf16[2,2,128,128]{3,2,1,0:T(8,128)(2,1)}, u32[]{:S(2)}, u32[]{:S(2)}) collective-permute-start(bf16[2,2,128,128]{3,2,1,0:T(8,128)(2,1)} %pad_maximum_fusion.15), channel_id=1, source_target_pairs={{0,4},{2,6},{4,0},{6,2},{8,12},{10,14},{12,8},{14,10},{16,20},{18,... | collective-permute-start | bytes 393224 | tf_op jit(solution)/shard_map/ppermute | solution.py:461
  7.7 0.6 copy-start.15
  8.3 1.2 copy-start.2
  9.5 0.9 copy-start.5
  10.5 0.8 copy-start.6
  11.2 10.2 %copy-start.13 = (bf16[256,128]{1,0:T(8,128)(2,1)S(1)}, bf16[256,128]{1,0:T(8,128)(2,1)}, u32[]{:S(2)}) copy-start(bf16[256,128]{1,0:T(8,128)(2,1)} %get-tuple-element.85) | copy-start | bytes 196612
  11.2 10.2 %copy-start.14 = (bf16[256,128]{1,0:T(8,128)(2,1)S(1)}, bf16[256,128]{1,0:T(8,128)(2,1)}, u32[]{:S(2)}) copy-start(bf16[256,128]{1,0:T(8,128)(2,1)} %get-tuple-element.112) | copy-start | bytes 196612
  11.2 10.9 %copy-start.10 = (bf16[256,2048]{1,0:T(8,128)(2,1)S(1)}, bf16[256,2048]{1,0:T(8,128)(2,1)}, u32[]{:S(2)}) copy-start(bf16[256,2048]{1,0:T(8,128)(2,1)} %param.12) | copy-start | bytes 3145732
  18.8 1.3 %copy-start = (f32[256,2048]{1,0:T(8,128)}, f32[256,2048]{1,0:T(8,128)S(1)}, u32[]{:S(2)}) copy-start(f32[256,2048]{1,0:T(8,128)S(1)} %get-tuple-element.19.mixed_ref) | copy-start | bytes 6291460
  20.1 3.3 %copy-start.11 = (bf16[256,128]{1,0:T(8,128)(2,1)S(1)}, bf16[256,128]{1,0:T(8,128)(2,1)}, u32[]{:S(2)}) copy-start(bf16[256,128]{1,0:T(8,128)(2,1)} %get-tuple-element.83) | copy-start | bytes 196612
  20.1 3.3 %copy-start.12 = (bf16[256,128]{1,0:T(8,128)(2,1)S(1)}, bf16[256,128]{1,0:T(8,128)(2,1)}, u32[]{:S(2)}) copy-start(bf16[256,128]{1,0:T(8,128)(2,1)} %get-tuple-element.114) | copy-start | bytes 196612
  21.2 12.8 %collective-permute-start.8 = (f32[2,136,1024]{2,1,0:T(8,128)}, f32[2,136,1024]{2,1,0:T(8,128)}, u32[]{:S(2)}, u32[]{:S(2)}) collective-permute-start(f32[2,136,1024]{2,1,0:T(8,128)} %constant_dynamic-slice_fusion), channel_id=1, source_target_pairs={{0,2},{2,0},{4,6},{6,4},{8,10},{10,8},{12,14},{14,12},{16,18},{18,... | collective-permute-start | bytes 3342344 | tf_op jit(solution)/shard_map/ppermute | solution.py:461
  22.1 5.7 %collective-permute-start.4 = (bf16[2,2,128,128]{3,2,1,0:T(8,128)(2,1)}, bf16[2,2,128,128]{3,2,1,0:T(8,128)(2,1)}, u32[]{:S(2)}, u32[]{:S(2)}) collective-permute-start(bf16[2,2,128,128]{3,2,1,0:T(8,128)(2,1)} %pad_maximum_fusion.16), channel_id=1, source_target_pairs={{0,6},{2,4},{4,2},{6,0},{8,14},{10,12},{12,10},{14,8},{16,22},{18,... | collective-permute-start | bytes 393224 | tf_op jit(solution)/shard_map/ppermute | solution.py:461
  23.0 10.5 %collective-permute-start = (bf16[256,1024]{1,0:T(8,128)(2,1)}, bf16[256,1024]{1,0:T(8,128)(2,1)S(1)}, u32[]{:S(2)}, u32[]{:S(2)}) collective-permute-start(bf16[256,1024]{1,0:T(8,128)(2,1)} %constant_dynamic-slice_fusion.10), channel_id=1, source_target_pairs={{0,2},{2,0},{4,6},{6,4},{8,10},{10,8},{12,14},{14,12},{16,18},{18,... | collective-permute-start | bytes 1572872 | tf_op jit(solution)/shard_map/ppermute | solution.py:461
  29.0 32.3 %collective-permute-start.7 = (bf16[2,4,2,128,128]{4,3,2,1,0:T(8,128)(2,1)S(1)}, bf16[2,4,2,128,128]{4,3,2,1,0:T(8,128)(2,1)S(1)}, u32[]{:S(2)}, u32[]{:S(2)}) collective-permute-start(bf16[2,4,2,128,128]{4,3,2,1,0:T(8,128)(2,1)S(1)} %pad_maximum_fusion.5.refs_4_), channel_id=1, source_target_pairs={{0,8},{2,10},{4,12},{6,14},{8,0},{10,2},{12,4},{14,6},{16,24},{18,... | collective-permute-start | bytes 1572872 | tf_op jit(solution)/shard_map/ppermute | solution.py:461
  30.6 38.2 %collective-permute-start.6 = (bf16[2,4,2,128,128]{4,3,2,1,0:T(8,128)(2,1)S(1)}, bf16[2,4,2,128,128]{4,3,2,1,0:T(8,128)(2,1)S(1)}, u32[]{:S(2)}, u32[]{:S(2)}) collective-permute-start(bf16[2,4,2,128,128]{4,3,2,1,0:T(8,128)(2,1)S(1)} %pad_maximum_fusion.5.refs_4_), channel_id=1, source_target_pairs={{0,16},{2,18},{4,20},{6,22},{8,24},{10,26},{12,28},{14,30},{16,0},... | collective-permute-start | bytes 1572872 | tf_op jit(solution)/shard_map/ppermute | solution.py:461
  33.2 45.5 %collective-permute-start.5 = (bf16[2,4,2,128,128]{4,3,2,1,0:T(8,128)(2,1)S(1)}, bf16[2,4,2,128,128]{4,3,2,1,0:T(8,128)(2,1)S(1)}, u32[]{:S(2)}, u32[]{:S(2)}) collective-permute-start(bf16[2,4,2,128,128]{4,3,2,1,0:T(8,128)(2,1)S(1)} %pad_maximum_fusion.5.refs_4_), channel_id=1, source_target_pairs={{0,24},{2,26},{4,28},{6,30},{8,16},{10,18},{12,20},{14,22},{16,8},... | collective-permute-start | bytes 1572872 | tf_op jit(solution)/shard_map/ppermute | solution.py:461
  33.5 14.9 %collective-permute-start.1 = (bf16[2,256,512]{2,1,0:T(8,128)(2,1)S(1)}, bf16[2,256,512]{2,1,0:T(8,128)(2,1)S(1)}, u32[]{:S(2)}, u32[]{:S(2)}) collective-permute-start(bf16[2,256,512]{2,1,0:T(8,128)(2,1)S(1)} %pad_maximum_fusion.4), channel_id=1, source_target_pairs={{0,4},{2,6},{4,0},{6,2},{8,12},{10,14},{12,8},{14,10},{16,20},{18,... | collective-permute-start | bytes 1572872 | tf_op jit(solution)/shard_map/ppermute | solution.py:461
  35.5 1.0 copy-start.8
  35.5 1.4 %copy-start.9 = (f32[2,136,1024]{2,1,0:T(8,128)}, f32[2,136,1024]{2,1,0:T(8,128)S(1)}, u32[]{:S(2)}) copy-start(f32[2,136,1024]{2,1,0:T(8,128)S(1)} %get-tuple-element.39) | copy-start | bytes 3342340
  36.9 23.1 %collective-permute-start.9 = (bf16[2,144,512]{2,1,0:T(8,128)(2,1)S(1)}, bf16[2,144,512]{2,1,0:T(8,128)(2,1)S(1)}, u32[]{:S(2)}, u32[]{:S(2)}) collective-permute-start(bf16[2,144,512]{2,1,0:T(8,128)(2,1)S(1)} %fusion.16), channel_id=1, source_target_pairs={{0,4},{2,6},{4,0},{6,2},{8,12},{10,14},{12,8},{14,10},{16,20},{18,... | collective-permute-start | bytes 884744 | tf_op jit(solution)/shard_map/ppermute | solution.py:461
  60.6 14.8 %collective-permute-start.10 = (bf16[2,144,512]{2,1,0:T(8,128)(2,1)S(1)}, bf16[2,144,512]{2,1,0:T(8,128)(2,1)S(1)}, u32[]{:S(2)}, u32[]{:S(2)}) collective-permute-start(bf16[2,144,512]{2,1,0:T(8,128)(2,1)S(1)} %pad_maximum_fusion.10), channel_id=1, source_target_pairs={{0,8},{2,10},{4,12},{6,14},{8,0},{10,2},{12,4},{14,6},{16,24},{18,... | collective-permute-start | bytes 884744 | tf_op jit(solution)/shard_map/ppermute | solution.py:461
  76.1 15.7 %collective-permute-start.11 = (bf16[2,144,512]{2,1,0:T(8,128)(2,1)S(1)}, bf16[2,144,512]{2,1,0:T(8,128)(2,1)S(1)}, u32[]{:S(2)}, u32[]{:S(2)}) collective-permute-start(bf16[2,144,512]{2,1,0:T(8,128)(2,1)S(1)} %pad_maximum_fusion.11), channel_id=1, source_target_pairs={{0,16},{2,18},{4,20},{6,22},{8,24},{10,26},{12,28},{14,30},{16,0},... | collective-permute-start | bytes 884744 | tf_op jit(solution)/shard_map/ppermute | solution.py:461
  92.9 9.6 %collective-permute-start.16 = (bf16[2,128,512]{2,1,0:T(8,128)(2,1)}, bf16[2,128,512]{2,1,0:T(8,128)(2,1)}, u32[]{:S(2)}, u32[]{:S(2)}) collective-permute-start(bf16[2,128,512]{2,1,0:T(8,128)(2,1)} %broadcast_select_fusion.10), channel_id=1, source_target_pairs={{0,4},{2,6},{4,0},{6,2},{8,12},{10,14},{12,8},{14,10},{16,20},{18,... | collective-permute-start | bytes 786440 | tf_op jit(solution)/shard_map/ppermute | solution.py:461
  94.6 16.0 %slice-start = ((s8[8388608]{0:T(1024)(128)(4,1)}), s8[4194304]{0:T(1024)(128)(4,1)S(1)}, s32[]{:S(2)}) async-start(s8[8388608]{0:T(1024)(128)(4,1)} %bitcast.174), calls=%async_computation | async-start | bytes 8388608
  95.0 13.0 %collective-permute-start.12 = (bf16[256,512]{1,0:T(8,128)(2,1)S(1)}, bf16[256,512]{1,0:T(8,128)(2,1)S(1)}, u32[]{:S(2)}, u32[]{:S(2)}) collective-permute-start(bf16[256,512]{1,0:T(8,128)(2,1)S(1)} %get-tuple-element.58), channel_id=1, source_target_pairs={{0,4},{2,6},{4,0},{6,2},{8,12},{10,14},{12,8},{14,10},{16,20},{18,... | collective-permute-start | bytes 786440 | tf_op jit(solution)/shard_map/ppermute | solution.py:461
  96.5 11.4 %collective-permute-start.13 = (bf16[256,512]{1,0:T(8,128)(2,1)S(1)}, bf16[256,512]{1,0:T(8,128)(2,1)S(1)}, u32[]{:S(2)}, u32[]{:S(2)}) collective-permute-start(bf16[256,512]{1,0:T(8,128)(2,1)S(1)} %get-tuple-element.60), channel_id=1, source_target_pairs={{0,2},{2,0},{4,6},{6,4},{8,10},{10,8},{12,14},{14,12},{16,18},{18,... | collective-permute-start | bytes 786440 | tf_op jit(solution)/shard_map/ppermute | solution.py:461
  96.5 13.8 %collective-permute-start.14 = (bf16[256,512]{1,0:T(8,128)(2,1)S(1)}, bf16[256,512]{1,0:T(8,128)(2,1)S(1)}, u32[]{:S(2)}, u32[]{:S(2)}) collective-permute-start(bf16[256,512]{1,0:T(8,128)(2,1)S(1)} %get-tuple-element.59), channel_id=1, source_target_pairs={{0,6},{2,4},{4,2},{6,0},{8,14},{10,12},{12,10},{14,8},{16,22},{18,... | collective-permute-start | bytes 786440 | tf_op jit(solution)/shard_map/ppermute | solution.py:461
  103.6 7.0 %slice-start.1 = ((s8[8388608]{0:T(1024)(128)(4,1)}), s8[4194304]{0:T(1024)(128)(4,1)S(1)}, s32[]{:S(2)}) async-start(s8[8388608]{0:T(1024)(128)(4,1)} %bitcast.174), calls=%async_computation.1 | async-start | bytes 8388608
  105.3 9.4 %collective-permute-start.17 = (bf16[2,128,1024]{2,1,0:T(8,128)(2,1)S(1)}, bf16[2,128,1024]{2,1,0:T(8,128)(2,1)S(1)}, u32[]{:S(2)}, u32[]{:S(2)}) collective-permute-start(bf16[2,128,1024]{2,1,0:T(8,128)(2,1)S(1)} %broadcast_select_fusion.2), channel_id=1, source_target_pairs={{0,2},{2,0},{4,6},{6,4},{8,10},{10,8},{12,14},{14,12},{16,18},{18,... | collective-permute-start | bytes 1572872 | tf_op jit(solution)/shard_map/ppermute | solution.py:461
  111.9 14.5 %collective-permute-start.15 = (bf16[256,1024]{1,0:T(8,128)(2,1)S(1)}, bf16[256,1024]{1,0:T(8,128)(2,1)S(1)}, u32[]{:S(2)}, u32[]{:S(2)}) collective-permute-start(bf16[256,1024]{1,0:T(8,128)(2,1)S(1)} %fusion.4), channel_id=1, source_target_pairs={{0,1},{1,0},{2,3},{3,2},{4,5},{5,4},{6,7},{7,6},{8,9},{9,8},{10,11... | collective-permute-start | bytes 1572872 | tf_op jit(solution)/shard_map/ppermute | solution.py:645
  114.7 1.6 %copy-start.1 = (f32[256,2048]{1,0:T(8,128)S(1)}, f32[256,2048]{1,0:T(8,128)}, u32[]{:S(2)}) copy-start(f32[256,2048]{1,0:T(8,128)} %copy-done) | copy-start | bytes 6291460
  114.7 1.8 %copy-start.3 = (bf16[256,2048]{1,0:T(8,128)(2,1)S(1)}, bf16[256,2048]{1,0:T(8,128)(2,1)}, u32[]{:S(2)}) copy-start(bf16[256,2048]{1,0:T(8,128)(2,1)} %gate_ref.1) | copy-start | bytes 3145732
  114.8 1.8 %copy-start.7 = (f32[2048]{0:T(1024)S(1)}, f32[2048]{0:T(1024)}, u32[]{:S(2)}) copy-start(f32[2048]{0:T(1024)} %param.22) | copy-start | bytes 24580
